TPU v7x, 32 devices: a whole 2x2x4 slice. The times are simulated.
32 devices in a mesh: seq: 2 (over core), ctx: 8 (over z, y), fsdp: 2 (over x).
Axes of the slice: x: 2, y: 2, z: 4, core: 2. Of those that a mesh axis runs over, the one named last changes fastest.
Arguments:
- tokens: bfloat16 [4, 1024, 1024], P(('seq', 'fsdp'), 'ctx'), may hold values from -6 to 6
- qkv_weight: bfloat16 [1024, 3072], P(('seq', 'ctx', 'fsdp')), may hold values from -0.3125 to 0.3125
- out_weight: bfloat16 [1024, 1024], P(('seq', 'ctx', 'fsdp')), may hold values from -0.1875 to 0.1875
- up_weight: bfloat16 [1024, 4096], P(('seq', 'ctx', 'fsdp')), may hold values from -0.1875 to 0.1875
- down_weight: bfloat16 [4096, 1024], P(('seq', 'ctx', 'fsdp')), may hold values from -0.09375 to 0.09375
- query_bias: bfloat16 [1024], P(('seq', 'ctx', 'fsdp')), may hold values from -3 to 3
- value_bias: bfloat16 [1024], P(('seq', 'ctx', 'fsdp')), may hold values from -3 to 3
- out_bias: bfloat16 [1024], P(('seq', 'ctx', 'fsdp')), may hold values from -3 to 3
- up_bias: bfloat16 [4096], P(('seq', 'ctx', 'fsdp')), may hold values from -3 to 3
- down_bias: bfloat16 [1024], P(('seq', 'ctx', 'fsdp')), may hold values from -3 to 3
- norm1_gain: bfloat16 [1024], P(('seq', 'ctx', 'fsdp')), may hold values from 0.25 to 1.75
- norm1_bias: bfloat16 [1024], P(('seq', 'ctx', 'fsdp')), may hold values from -3 to 3
- norm2_gain: bfloat16 [1024], P(('seq', 'ctx', 'fsdp')), may hold values from 0.25 to 1.75
- norm2_bias: bfloat16 [1024], P(('seq', 'ctx', 'fsdp')), may hold values from -3 to 3
- cotangent: bfloat16 [4, 1024, 1024], P(('seq', 'fsdp'), 'ctx'), may hold values from -6 to 6
Outputs:
- output: bfloat16 [4, 1024, 1024], P(('seq', 'fsdp'), 'ctx')
- input_grad: float32 [4, 1024, 1024], P(('seq', 'fsdp'), 'ctx')
- qkv_weight_grad: float32 [1024, 3072], P(('seq', 'ctx', 'fsdp'))
- out_weight_grad: float32 [1024, 1024], P(('seq', 'ctx', 'fsdp'))
- up_weight_grad: float32 [1024, 4096], P(('seq', 'ctx', 'fsdp'))
- down_weight_grad: float32 [4096, 1024], P(('seq', 'ctx', 'fsdp'))
- query_bias_gradient: float32 [1024], P(('seq', 'ctx', 'fsdp'))
- value_bias_grad: float32 [1024], P(('seq', 'ctx', 'fsdp'))
- out_bias_grad: float32 [1024], P(('seq', 'ctx', 'fsdp'))
- up_bias_grad: float32 [4096], P(('seq', 'ctx', 'fsdp'))
- down_bias_grad: float32 [1024], P(('seq', 'ctx', 'fsdp'))
- norm1_gain_grad: float32 [1024], P(('seq', 'ctx', 'fsdp'))
- norm1_bias_grad: float32 [1024], P(('seq', 'ctx', 'fsdp'))
- norm2_gain_grad: float32 [1024], P(('seq', 'ctx', 'fsdp'))
- norm2_bias_grad: float32 [1024], P(('seq', 'ctx', 'fsdp'))
All inputs are finite; a program needn't handle non-finite values.
Results may differ from a plain program's by a relative error of at most 0.019.
The roundings to bfloat16 on the way count: a program that leaves them out, or rounds other values in their place, can miss the bound.
Values may be sent and summed in bfloat16 or wider, within the bound.
A program may use at most 192 MiB of HBM per device.

v0:
```python
import math

import jax
import jax.numpy as jnp
from jax import lax
from jax.sharding import PartitionSpec as P

HEADS = 16
HEAD_DIM = 64


epsilon = 1e-05


def split_blocks(piece):
    rows = piece.shape[0]
    block = math.gcd(rows, 512)
    return (piece.reshape(rows // block, block, HEADS, HEAD_DIM), block)


def norm_forward(values, gain, shift):
    centered = values - jnp.mean(values, axis=-1, keepdims=True)
    recip = lax.rsqrt(jnp.mean(centered * centered, axis=-1, keepdims=True) + epsilon)
    normal = centered * recip
    return (normal * gain + shift, normal, recip)


def norm_backward(upstream, normal, recip, gain):
    gain_grad = jnp.sum(upstream * normal, axis=0)
    shift_grad = jnp.sum(upstream, axis=0)
    scaled = upstream * gain
    inner = (
        scaled
        - jnp.mean(scaled, axis=-1, keepdims=True)
        - normal * jnp.mean(scaled * normal, axis=-1, keepdims=True)
    )
    return (recip * inner, gain_grad, shift_grad)


def matmul(left_neighbor, right_neighbor):
    return jnp.dot(left_neighbor, right_neighbor, preferred_element_type=jnp.float32)


def on_device(
    tokens,
    qkv_weight,
    out_weight,
    up_weight,
    down_weight,
    query_bias,
    value_bias,
    out_bias,
    up_bias,
    down_bias,
    norm1_gain,
    norm1_bias,
    norm2_gain,
    norm2_bias,
    cotangent,
):
    gathered = (
        lax.all_gather(qkv_weight, ("seq", "ctx", "fsdp"), axis=0, tiled=True),
        lax.all_gather(out_weight, ("seq", "ctx", "fsdp"), axis=0, tiled=True),
        lax.all_gather(up_weight, ("seq", "ctx", "fsdp"), axis=0, tiled=True),
        lax.all_gather(down_weight, ("seq", "ctx", "fsdp"), axis=0, tiled=True),
        lax.all_gather(query_bias, ("seq", "ctx", "fsdp"), axis=0, tiled=True),
        lax.all_gather(value_bias, ("seq", "ctx", "fsdp"), axis=0, tiled=True),
        lax.all_gather(out_bias, ("seq", "ctx", "fsdp"), axis=0, tiled=True),
        lax.all_gather(up_bias, ("seq", "ctx", "fsdp"), axis=0, tiled=True),
        lax.all_gather(down_bias, ("seq", "ctx", "fsdp"), axis=0, tiled=True),
        lax.all_gather(norm1_gain, ("seq", "ctx", "fsdp"), axis=0, tiled=True),
        lax.all_gather(norm1_bias, ("seq", "ctx", "fsdp"), axis=0, tiled=True),
        lax.all_gather(norm2_gain, ("seq", "ctx", "fsdp"), axis=0, tiled=True),
        lax.all_gather(norm2_bias, ("seq", "ctx", "fsdp"), axis=0, tiled=True),
    )
    qkv_full, out_full, up_full, down_full = (gathered[0], gathered[1], gathered[2], gathered[3])
    small = tuple((item.astype(jnp.float32) for item in gathered[4:]))
    q_shift, v_shift, o_shift, u_shift, d_shift, gain_one, shift_one, gain_two, shift_two = small
    scale = HEAD_DIM ** (-0.5)
    inputs = tokens[0]
    rows = inputs.shape[0]
    width = inputs.shape[1]
    joined_bias = jnp.concatenate([q_shift, jnp.zeros_like(q_shift), v_shift])
    qkv_low = (matmul(inputs, qkv_full) + joined_bias).astype(jnp.bfloat16)
    queries = qkv_low[:, :width].reshape(rows, HEADS, HEAD_DIM)
    keys_own = qkv_low[:, width : 2 * width]
    values_own = qkv_low[:, 2 * width :]
    start_state = (
        jnp.full((HEADS, rows), -1e30, jnp.float32),
        jnp.zeros((HEADS, rows), jnp.float32),
        jnp.zeros((rows, HEADS, HEAD_DIM), jnp.float32),
    )
    piece = (
        lax.all_gather(keys_own, "ctx", axis=0, tiled=True),
        lax.all_gather(values_own, "ctx", axis=0, tiled=True),
    )
    key_blocks, block = split_blocks(piece[0])
    value_blocks, block = split_blocks(piece[1])

    def inner(state, pair):
        run_max, run_sum, accum = state
        key_tile_rows, value_block = pair
        scores = (
            jnp.einsum("qhe,khe->hqk", queries, key_tile_rows, preferred_element_type=jnp.float32)
            * scale
        )
        new_max = jnp.maximum(run_max, jnp.max(scores, axis=-1))
        factor = jnp.exp(run_max - new_max)
        weights = jnp.exp(scores - new_max[..., None])
        run_sum = run_sum * factor + jnp.sum(weights, axis=-1)
        accum = accum * factor.T[..., None] + jnp.einsum(
            "hqk,khe->qhe",
            weights.astype(jnp.bfloat16),
            value_block,
            preferred_element_type=jnp.float32,
        )
        return ((new_max, run_sum, accum), None)

    result, unused = lax.scan(inner, start_state, (key_blocks, value_blocks))
    run_max, run_sum, accum = result
    attended = accum / run_sum.T[..., None]
    log_total = run_max + jnp.log(run_sum)
    attended_low = attended.reshape(rows, width).astype(jnp.bfloat16)
    first_sum = inputs.astype(jnp.float32) + matmul(attended_low, out_full) + o_shift
    first_norm, normal_one, recip_one = norm_forward(first_sum, gain_one, shift_one)
    normed_low = first_norm.astype(jnp.bfloat16)
    hidden_pre = matmul(normed_low, up_full) + u_shift
    activated_full, gelu_pull = jax.vjp(lambda pre: jax.nn.gelu(pre, approximate=False), hidden_pre)
    activated = activated_full.astype(jnp.bfloat16)
    second_sum = first_norm + matmul(activated, down_full) + d_shift
    final, normal_two, recip_two = norm_forward(second_sum, gain_two, shift_two)
    upstream = cotangent[0].astype(jnp.float32)
    d_second, gain_two_grad, shift_two_grad = norm_backward(
        upstream, normal_two, recip_two, gain_two
    )
    d_feed = d_second.astype(jnp.bfloat16)
    down_grad = matmul(activated.T, d_feed)
    down_bias_grad = jnp.sum(d_feed.astype(jnp.float32), axis=0)
    d_hidden = gelu_pull(matmul(d_feed, down_full.T))[0].astype(jnp.bfloat16)
    up_grad = matmul(normed_low.T, d_hidden)
    up_bias_grad = jnp.sum(d_hidden.astype(jnp.float32), axis=0)
    first_input_gradient = d_second + matmul(d_hidden, up_full.T)
    d_sum_one, gain_one_grad, first_shift_gradient = norm_backward(
        first_input_gradient, normal_one, recip_one, gain_one
    )
    d_branch = d_sum_one.astype(jnp.bfloat16)
    out_grad = matmul(attended_low.T, d_branch)
    out_bias_grad = jnp.sum(d_branch.astype(jnp.float32), axis=0)
    d_attended = matmul(d_branch, out_full.T).astype(jnp.bfloat16).reshape(rows, HEADS, HEAD_DIM)
    delta = jnp.sum(d_attended.astype(jnp.float32) * attended, axis=-1).T
    total_rows = rows * lax.axis_size("ctx")
    zero_query = jnp.zeros((rows, HEADS, HEAD_DIM), jnp.float32)
    start_back = (zero_query, jnp.zeros((total_rows, 2 * width), jnp.float32))
    piece = (
        lax.all_gather(keys_own, "ctx", axis=0, tiled=True),
        lax.all_gather(values_own, "ctx", axis=0, tiled=True),
    )
    key_blocks, block = split_blocks(piece[0])
    value_blocks, block = split_blocks(piece[1])
    counter = jnp.arange(key_blocks.shape[0], dtype=jnp.int32)

    def inner(state, triple):
        key_tile_rows, value_block, number = triple
        scores = (
            jnp.einsum("qhe,khe->hqk", queries, key_tile_rows, preferred_element_type=jnp.float32)
            * scale
        )
        weights = jnp.exp(scores - log_total[..., None])
        d_probs = jnp.einsum(
            "qhe,khe->hqk", d_attended, value_block, preferred_element_type=jnp.float32
        )
        d_scores = (weights * (d_probs - delta[..., None]) * scale).astype(jnp.bfloat16)
        d_query = state[0] + jnp.einsum(
            "hqk,khe->qhe", d_scores, key_tile_rows, preferred_element_type=jnp.float32
        )
        d_key = jnp.einsum(
            "hqk,qhe->khe", d_scores, queries, preferred_element_type=jnp.float32
        ).reshape(block, width)
        d_value = jnp.einsum(
            "hqk,qhe->khe",
            weights.astype(jnp.bfloat16),
            d_attended,
            preferred_element_type=jnp.float32,
        ).reshape(block, width)
        offset = number * block
        current = lax.dynamic_slice_in_dim(state[1], offset, block, 0)
        updated = lax.dynamic_update_slice_in_dim(
            state[1], current + jnp.concatenate([d_key, d_value], axis=1), offset, 0
        )
        return ((d_query, updated), None)

    result, unused = lax.scan(inner, start_back, (key_blocks, value_blocks, counter))
    d_query = result[0].reshape(rows, width)
    summed = lax.psum_scatter(result[1], "ctx", scatter_dimension=0, tiled=True)
    d_key = summed[:, :width]
    d_value = summed[:, width:]
    d_qkv = jnp.concatenate([d_query, d_key, d_value], axis=1).astype(jnp.bfloat16)
    qkv_grad = matmul(inputs.T, d_qkv)
    d_qkv_wide = d_qkv.astype(jnp.float32)
    query_bias_gradient = jnp.sum(d_qkv_wide[:, :width], axis=0)
    value_bias_grad = jnp.sum(d_qkv_wide[:, 2 * width :], axis=0)
    input_grad = matmul(d_qkv, qkv_full.T) + d_sum_one
    sharded = (
        lax.psum_scatter(qkv_grad, ("seq", "ctx", "fsdp"), scatter_dimension=0, tiled=True),
        lax.psum_scatter(out_grad, ("seq", "ctx", "fsdp"), scatter_dimension=0, tiled=True),
        lax.psum_scatter(up_grad, ("seq", "ctx", "fsdp"), scatter_dimension=0, tiled=True),
        lax.psum_scatter(down_grad, ("seq", "ctx", "fsdp"), scatter_dimension=0, tiled=True),
        lax.psum_scatter(
            query_bias_gradient, ("seq", "ctx", "fsdp"), scatter_dimension=0, tiled=True
        ),
        lax.psum_scatter(value_bias_grad, ("seq", "ctx", "fsdp"), scatter_dimension=0, tiled=True),
        lax.psum_scatter(out_bias_grad, ("seq", "ctx", "fsdp"), scatter_dimension=0, tiled=True),
        lax.psum_scatter(up_bias_grad, ("seq", "ctx", "fsdp"), scatter_dimension=0, tiled=True),
        lax.psum_scatter(down_bias_grad, ("seq", "ctx", "fsdp"), scatter_dimension=0, tiled=True),
        lax.psum_scatter(gain_one_grad, ("seq", "ctx", "fsdp"), scatter_dimension=0, tiled=True),
        lax.psum_scatter(
            first_shift_gradient, ("seq", "ctx", "fsdp"), scatter_dimension=0, tiled=True
        ),
        lax.psum_scatter(gain_two_grad, ("seq", "ctx", "fsdp"), scatter_dimension=0, tiled=True),
        lax.psum_scatter(shift_two_grad, ("seq", "ctx", "fsdp"), scatter_dimension=0, tiled=True),
    )
    return (
        final.astype(jnp.bfloat16)[None],
        input_grad[None],
        sharded[0],
        sharded[1],
        sharded[2],
        sharded[3],
        sharded[4],
        sharded[5],
        sharded[6],
        sharded[7],
        sharded[8],
        sharded[9],
        sharded[10],
        sharded[11],
        sharded[12],
    )


def solution(mesh):
    placed = (
        P(("seq", "fsdp"), "ctx", None),
        P(("seq", "ctx", "fsdp"), None),
        P(("seq", "ctx", "fsdp"), None),
        P(("seq", "ctx", "fsdp"), None),
        P(("seq", "ctx", "fsdp"), None),
        P(("seq", "ctx", "fsdp")),
        P(("seq", "ctx", "fsdp")),
        P(("seq", "ctx", "fsdp")),
        P(("seq", "ctx", "fsdp")),
        P(("seq", "ctx", "fsdp")),
        P(("seq", "ctx", "fsdp")),
        P(("seq", "ctx", "fsdp")),
        P(("seq", "ctx", "fsdp")),
        P(("seq", "ctx", "fsdp")),
        P(("seq", "fsdp"), "ctx", None),
    )
    return jax.shard_map(
        on_device,
        mesh=mesh,
        in_specs=placed,
        out_specs=(
            P(("seq", "fsdp"), "ctx", None),
            P(("seq", "fsdp"), "ctx", None),
            P(("seq", "ctx", "fsdp"), None),
            P(("seq", "ctx", "fsdp"), None),
            P(("seq", "ctx", "fsdp"), None),
            P(("seq", "ctx", "fsdp"), None),
            P(("seq", "ctx", "fsdp")),
            P(("seq", "ctx", "fsdp")),
            P(("seq", "ctx", "fsdp")),
            P(("seq", "ctx", "fsdp")),
            P(("seq", "ctx", "fsdp")),
            P(("seq", "ctx", "fsdp")),
            P(("seq", "ctx", "fsdp")),
            P(("seq", "ctx", "fsdp")),
            P(("seq", "ctx", "fsdp")),
        ),
        check_vma=False,
    )
```

profile of v0, /device:TPU:1, one launch (start us, length us, event | category | flops | bytes accessed | tf_op | source)
XLA Modules:
  0.0 1644.4 jit_solution(15470390804989086014)
XLA Ops:
  8.0 0.8 dynamic-update-slice.7
  8.8 0.8 dynamic-update-slice.3
  9.7 0.8 dynamic-update-slice.4
  13.0 0.8 dynamic-update-slice.1
  13.8 0.8 dynamic-update-slice.6
  14.7 41.5 %all-reduce.18 = (bf16[1024]{0:T(1024)(128)(2,1)S(1)}, bf16[1024]{0:T(1024)(128)(2,1)S(1)}, bf16[1024]{0:T(1024)(128)(2,1)S(1)}, bf16[1024]{0:T(1024)(128)(2,1)S...) all-reduce(bf16[1024]{0:T(1024)(128)(2,1)S(1)} %dynamic-update-slic, ...), channel_id=1, replica_groups=mesh['seq'=2,'ctx'=8,'fsdp'=2] {'seq','ctx','fsdp'}, use_global_device_ids=true, to_apply=%add.1 | all-reduce | flops 8192 | bytes 32768
  56.3 26.9 %all-gather.8.cloned.1.call-done = bf16[1024,3072]{1,0:T(8,128)(2,1)} async-done(((bf16[32,3072]{1,0:T(8,128)(2,1)}), bf16[1024,3072]{1,0:T(8,128)(2,1)}) %all-gather.8.cloned.1.call-update) | async-done | bytes 6291472 | tf_op jit(solution)/shard_map/all_gather | solution.py:62
  83.2 3.9 fusion.41
  87.1 0.8 fusion.81
  90.6 65.6 %all-gather = bf16[32,1,128]{2,1,0:T(2,128)(2,1)S(1)} all-gather(bf16[1,1,128]{2,1,0:T(2,128)(2,1)S(1)} %bitcast.168), channel_id=1, replica_groups=mesh['seq'=2,'ctx'=8,'fsdp'=2] {'seq','ctx','fsdp'}, dimensions={0}, use_global_device_ids=true | all-gather | bytes 8448 | tf_op jit(solution)/shard_map/all_gather | solution.py:69
  156.4 6.4 reshape.140
  162.8 4.5 copy.54
  167.3 17.8 %all-gather.12.cloned.1.call-done = bf16[1024,1024]{1,0:T(8,128)(2,1)} async-done(((bf16[128,1024]{1,0:T(8,128)(2,1)}), bf16[1024,1024]{1,0:T(8,128)(2,1)}) %all-gather.12.cloned.1.call-update) | async-done | bytes 2097168 | tf_op jit(solution)/shard_map/all_gather | solution.py:95
  185.1 6.4 reshape.141
  191.4 5.5 copy.55
  196.9 7.3 while.28
  196.9 0.8 bitcast_reduce_fusion.2
  198.5 0.9 copy-done.1
  199.4 1.1 fusion.132
  200.5 0.8 bitcast_reduce_fusion.2
  202.1 0.9 copy-done.1
  202.9 1.1 fusion.132
  204.3 39.9 %all-gather.14.cloned.1.call-done = bf16[1024,1024]{1,0:T(8,128)(2,1)} async-done(((bf16[32,1024]{1,0:T(8,128)(2,1)}), bf16[1024,1024]{1,0:T(8,128)(2,1)}) %all-gather.14.cloned.1.call-update) | async-done | bytes 2097168 | tf_op jit(solution)/shard_map/all_gather | solution.py:63
  244.2 2.1 fusion.82
  247.4 76.0 %all-gather.16.cloned.1.call-done = bf16[1024,4096]{1,0:T(8,128)(2,1)} async-done(((bf16[32,4096]{1,0:T(8,128)(2,1)}), bf16[1024,4096]{1,0:T(8,128)(2,1)}) %all-gather.16.cloned.1.call-update) | async-done | bytes 8388624 | tf_op jit(solution)/shard_map/all_gather | solution.py:64
  323.4 6.3 convolution_add_fusion
  329.7 72.6 %all-gather.18.cloned.1.call-done = bf16[4096,1024]{1,0:T(8,128)(2,1)} async-done(((bf16[128,1024]{1,0:T(8,128)(2,1)}), bf16[4096,1024]{1,0:T(8,128)(2,1)}) %all-gather.18.cloned.1.call-update) | async-done | bytes 8388624 | tf_op jit(solution)/shard_map/all_gather | solution.py:65
  402.3 9.7 fusion.83
  412.5 1.0 convert_reduce_fusion.2
  413.6 7.7 convert_reduce_fusion
  421.4 3.1 multiply_reduce_fusion
  425.5 1.5 convolution_convert_fusion
  427.0 1.1 copy.56
  428.3 4.3 broadcast_in_dim.18
  432.6 25.0 %while.29 = (s32[]{:T(128)}, f32[128,16,64]{0,2,1:T(8,128)S(1)}, f32[1024,2048]{0,1:T(8,128)}, bf16[2,512,16,64]{1,3,2,0:T(8,128)(2,1)S(1)}, bf16[128,16,64]{0,2...) while((s32[]{:T(128)}, f32[128,16,64]{0,2,1:T(8,128)S(1)}, ...), condition=%wide.region_14.15_spmd.clone, body=%wide.region_13.14_spmd.clone.sunk | while | flops 682885120 | bytes 108028224 | solution.py:192
  435.4 1.5 multiply_convert_fusion.5
  436.9 0.9 fusion.145
  438.6 0.8 fusion.146
  439.4 1.2 slice-done.1
  440.6 1.3 fusion.147
  441.9 3.2 copy-done
  447.9 1.5 multiply_convert_fusion.5
  449.4 0.9 fusion.145
  451.1 0.8 fusion.146
  452.0 1.2 slice-done.1
  453.1 1.3 fusion.147
  454.4 3.2 copy-done
  457.7 1.0 copy-done.8
  458.7 2.6 fusion.68
  461.5 143.9 %reduce-scatter.8.cloned.1.call-done = f32[128,2048]{0,1:T(8,128)} async-done(((f32[1024,2048]{0,1:T(8,128)}), f32[128,2048]{0,1:T(8,128)}) %reduce-scatter.8.cloned.1.call-update) | async-done | bytes 1048592 | tf_op jit(solution)/shard_map/reduce_scatter | solution.py:194
  605.4 1.3 convert.8
  606.7 6.4 convolution_bitcast_fusion.1
  613.0 12.8 copy.61
  625.9 1.0 copy-done.19
  626.9 10.9 fusion.71
  637.9 1.0 copy-done.5
  639.3 8.2 fusion.77
  647.5 0.9 copy-done.14
  648.9 42.4 %all-reduce.17 = (f32[1024]{0:T(1024)S(1)}, f32[1024]{0:T(1024)S(1)}, f32[1024]{0:T(1024)S(1)}, f32[4096]{0:T(1024)S(1)}, f32[1024]{0:T(1024)S(1)}, /*index=5*/f...) all-reduce(f32[1024]{0:T(1024)S(1)} %get-tuple-element.266, ...), channel_id=7, replica_groups=mesh['seq'=2,'ctx'=8,'fsdp'=2] {'seq','ctx','fsdp'}, use_global_device_ids=true, to_apply=%region_21.22.clone | all-reduce | flops 12288 | bytes 98304
  696.5 5.8 fusion.50
  702.3 52.2 %reduce-scatter.10.cloned.1.call-done = f32[32,1024]{1,0:T(8,128)} async-done(((f32[1024,1024]{1,0:T(8,128)}), f32[32,1024]{1,0:T(8,128)}) %reduce-scatter.10.cloned.1.call-update) | async-done | bytes 131088 | tf_op jit(solution)/shard_map/reduce_scatter | solution.py:205
  754.6 159.3 %reduce-scatter.16.cloned.1.call-done = f32[32,3072]{1,0:T(8,128)} async-done(((f32[1024,3072]{1,0:T(8,128)}), f32[32,3072]{1,0:T(8,128)}) %reduce-scatter.16.cloned.1.call-update) | async-done | bytes 393232
  913.8 360.8 %reduce-scatter.14.cloned.1.call-done = f32[128,1024]{1,0:T(8,128)} async-done(((f32[4096,1024]{1,0:T(8,128)}), f32[128,1024]{1,0:T(8,128)}) %reduce-scatter.14.cloned.1.call-update) | async-done | bytes 524304 | tf_op jit(solution)/shard_map/reduce_scatter | solution.py:207
  1274.6 362.9 %reduce-scatter.12.cloned.1.call-done = f32[32,4096]{1,0:T(8,128)} async-done(((f32[1024,4096]{1,0:T(8,128)}), f32[32,4096]{1,0:T(8,128)}) %reduce-scatter.12.cloned.1.call-update) | async-done | bytes 524304 | tf_op jit(solution)/shard_map/reduce_scatter | solution.py:206
  (147 shorter events, 22.5 us)
Async XLA Ops:
  7.2 76.0 %all-gather.8.cloned.1.call-start = ((), (), s32[]{:S(2)}) async-start(), calls=%async_computation.5 | async-start | bytes 6488064 | tf_op jit(solution)/shard_map/all_gather | solution.py:62
  7.9 148.5 %all-gather.10.cloned.1.call-start = ((), (), s32[]{:S(2)}) async-start(), calls=%async_computation.6 | async-start | bytes 2359296 | tf_op jit(solution)/shard_map/all_gather | solution.py:94
  87.1 3.5 copy-start.20
  87.9 97.1 %all-gather.12.cloned.1.call-start = ((), (), s32[]{:S(2)}) async-start(), calls=%async_computation.7 | async-start | bytes 2359296 | tf_op jit(solution)/shard_map/all_gather | solution.py:95
  88.7 155.6 %all-gather.14.cloned.1.call-start = ((), (), s32[]{:S(2)}) async-start(), calls=%async_computation.8 | async-start | bytes 2162688 | tf_op jit(solution)/shard_map/all_gather | solution.py:63
  89.2 234.2 %all-gather.16.cloned.1.call-start = ((), (), s32[]{:S(2)}) async-start(), calls=%async_computation.9 | async-start | bytes 8650752 | tf_op jit(solution)/shard_map/all_gather | solution.py:64
  89.8 312.5 %all-gather.18.cloned.1.call-start = ((), (), s32[]{:S(2)}) async-start(), calls=%async_computation.10 | async-start | bytes 8650752 | tf_op jit(solution)/shard_map/all_gather | solution.py:65
  90.4 515.0 %reduce-scatter.8.cloned.1.call-start = ((), (), s32[]{:S(2)}) async-start(), calls=%async_computation.11 | async-start | bytes 9437184 | tf_op jit(solution)/shard_map/reduce_scatter | solution.py:194
  196.9 47.3 %copy-start.12 = (bf16[1,128,1024]{2,1,0:T(8,128)(2,1)S(1)}, bf16[1,128,1024]{2,1,0:T(8,128)(2,1)}, u32[]{:S(2)}) copy-start(bf16[1,128,1024]{2,1,0:T(8,128)(2,1)} %param.19) | copy-start | bytes 786436
  197.8 1.6 copy-start.1
  201.3 1.6 copy-start.1
  204.3 119.1 %copy-start.15 = (bf16[128,16,64]{0,2,1:T(8,128)(2,1)}, bf16[128,16,64]{0,2,1:T(8,128)(2,1)S(1)}, u32[]{:S(2)}) copy-start(bf16[128,16,64]{0,2,1:T(8,128)(2,1)S(1)} %fusion.65) | copy-start | bytes 786436
  246.4 0.8 copy-start.3
  329.7 82.6 %copy-start.13 = (bf16[1,128,1024]{2,1,0:T(8,128)(2,1)S(1)}, bf16[1,128,1024]{2,1,0:T(8,128)(2,1)}, u32[]{:S(2)}) copy-start(bf16[1,128,1024]{2,1,0:T(8,128)(2,1)} %param.33) | copy-start | bytes 786436
  402.3 11.2 copy-start.21
  412.0 1.6 copy-start.17
  412.2 9.1 slice-start.2
  413.5 7.8 copy-start.18
  413.6 7.7 slice-start.3
  413.6 7.8 copy-start.4
  421.3 3.1 copy-start.10
  421.4 4.1 copy-start.9
  424.7 0.8 copy-start.7
  428.3 4.3 copy-start.6
  433.8 1.6 copy-start.2
  436.9 2.5 slice-start
  437.8 2.8 slice-start.1
  441.9 3.2 copy-start
  446.3 1.6 copy-start.2
  449.4 2.5 slice-start
  450.4 2.8 slice-start.1
  454.4 3.2 copy-start
  457.6 1.0 copy-start.8
  457.6 1.1 copy-start.16
  457.6 296.9 %reduce-scatter.10.cloned.1.call-start = ((), (), s32[]{:S(2)}) async-start(), calls=%async_computation.12 | async-start | bytes 4325376 | tf_op jit(solution)/shard_map/reduce_scatter | solution.py:205
  461.4 452.4 %reduce-scatter.16.cloned.1.call-start = ((), (), s32[]{:S(2)}) async-start(), calls=%async_computation.15 | async-start | bytes 12976128
  625.9 1.0 copy-start.19
  625.9 648.7 %reduce-scatter.14.cloned.1.call-start = ((), (), s32[]{:S(2)}) async-start(), calls=%async_computation.14 | async-start | bytes 17301504 | tf_op jit(solution)/shard_map/reduce_scatter | solution.py:207
  637.9 1.0 copy-start.5
  637.9 1.4 copy-start.11
  637.9 999.6 %reduce-scatter.12.cloned.1.call-start = ((), (), s32[]{:S(2)}) async-start(), calls=%async_computation.13 | async-start | bytes 17301504 | tf_op jit(solution)/shard_map/reduce_scatter | solution.py:206
  647.4 1.0 copy-start.14
Sparse Core Ops, SparseCore 0:
  10.9 72.2 all-gather.7
  88.0 46.4 all-gather.9
  137.3 47.7 all-gather.11
  187.8 56.4 all-gather.13
  247.0 76.3 all-gather.15
  326.1 76.1 all-gather.17
  457.8 147.6 reduce-scatter.7
  608.4 146.1 reduce-scatter.9
  762.2 151.5 reduce-scatter.15
  916.5 357.9 reduce-scatter.13
  1277.5 359.9 reduce-scatter.11
where the time goes:
time: 1650 us; the launch traced here: 1640 us
  waiting for transfers between devices  1320 us (80%)
  blocking collectives  150 us (9%)
  matrix products  81.6 us (5%)
  local copies, waits for them, and re-layouts  73.1 us (4%)
    reduce_scatter x1, waiting for transfers between devices, on_device(): lax.psum_scatter(up_grad, ('seq', 'ctx', 'fsdp'), scatter_dimension=0, ti...  363 us
    reduce_scatter x1, waiting for transfers between devices, on_device(): lax.psum_scatter(down_grad, ('seq', 'ctx', 'fsdp'), scatter_dimension=0,...  361 us
    unnamed x12, waiting for transfers between devices  162 us
    reduce_scatter x1, waiting for transfers between devices, on_device(): summed = lax.psum_scatter(result[1], 'ctx', scatter_dimension=0, tiled=True)  144 us
    unnamed x2, blocking collectives  83.9 us
    all_gather x1, waiting for transfers between devices, on_device(): lax.all_gather(up_weight, ('seq', 'ctx', 'fsdp'), axis=0, tiled=True)  76 us
    all_gather x1, waiting for transfers between devices, on_device(): lax.all_gather(down_weight, ('seq', 'ctx', 'fsdp'), axis=0, tiled=True)  72.6 us
    dot_general x12, matrix products, matmul(): jnp.dot(left_neighbor, right_neighbor, preferred_element_type=jnp.float32)  68.2 us
  transfers between devices with their start and end apart: 11, of which 10 were waited for; matrix products, arithmetic and copies ran while one was open for 6% of the time, Pallas kernels for 0%

commit v1 on v0

--- a/solution.py
+++ b/solution.py
@@ -1,8 +1,12 @@
+import functools
+import itertools
 import math
 
 import jax
 import jax.numpy as jnp
 from jax import lax
+from jax.experimental import pallas as pl
+from jax.experimental.pallas import tpu as pltpu
 from jax.sharding import PartitionSpec as P
 
 HEADS = 16
@@ -10,6 +14,10 @@
 
 
 epsilon = 1e-05
+MESH = pl.DeviceIdType.MESH
+F32 = jnp.float32
+BF16 = jnp.bfloat16
+TILE = 256
 
 
 def split_blocks(piece):
@@ -238,6 +246,795 @@
     )
 
 
+def dot(left, right, left_dim=1, right_dim=0):
+    return lax.dot_general(
+        left, right, (((left_dim,), (right_dim,)), ((), ())), preferred_element_type=F32
+    )
+
+
+def loop(count, body):
+    def step(i, carry):
+        body(i)
+        return carry
+
+    lax.fori_loop(0, count, step, 0)
+
+
+def spread_matrix(width, piece, at):
+    lane = lax.broadcasted_iota(jnp.int32, (128, width), 0)
+    column = lax.broadcasted_iota(jnp.int32, (128, width), 1)
+    return jnp.where(lane == at * piece + column % piece, 1.0, 0.0)
+
+
+def own_columns(blocks, width):
+    row = lax.broadcasted_iota(jnp.int32, (blocks, width), 0)
+    column = lax.broadcasted_iota(jnp.int32, (blocks, width), 1)
+    return column // (width // blocks) == row
+
+
+def layer_kernel(
+    tok, qkvw, outw, upw, downw, pack, cot,
+    out_o, ig_o, qkvg_o, outg_o, upg_o, downg_o, small_o,
+    X16, WP, WH, G, OW, UW, DW,
+    QN, KN, VN, QKVT, OT, OTB, LSE, AS, AT, A4,
+    R1A, R1B, R1C, R1D, R2A, R2B, R2C, R2D, KR,
+    N4, N4T, C4, C4T, GP, DF4,
+    FN, NORM1, DSEC,
+    DS, DR, DA, DAT, DKV, DQT, DQKV, DQKVT,
+    USA, URA, USB, URB, USC, URC, UK, UF,
+    DSA, DRA, DSB, DRB, DSC, DRC, DK,
+    OSA, ORA, OSB, ORB, OSC, ORC, OK,
+    IRA, ISB, IRB, ISC, IRC, ISD, IRD, IK,
+    QSA, QRA, QK, QSB, QG,
+    VEC, UB, VG, SG, RG,
+    ssem, rsem, wss, wrs, gss, grs, hss, hrs,
+):
+    s = lax.axis_index("seq")
+    c = lax.axis_index("ctx")
+    x = lax.axis_index("fsdp")
+    h, l, y = c // 4, (c // 2) % 2, c % 2
+    here = {"s": s, "h": h, "l": l, "y": y, "x": x}
+    me = s * 16 + c * 2 + x
+    head = s * 8 + c
+    width = tok.shape[1]
+    tiles = width // TILE
+    counter = itertools.count()
+    sends = []
+
+    def at(flips):
+        return {k: (1 - v if k in flips else v) for k, v in here.items()}
+
+    def device(flips):
+        p = at(flips)
+        return {"seq": p["s"], "ctx": p["h"] * 4 + p["l"] * 2 + p["y"], "fsdp": p["x"]}
+
+    def ids(n=1):
+        return [next(counter) for _ in range(n)][0]
+
+    def copy(src, dst, sem, flips):
+        return pltpu.make_async_remote_copy(
+            src_ref=src, dst_ref=dst, send_sem=ssem.at[sem], recv_sem=rsem.at[sem],
+            device_id=device(flips), device_id_type=MESH,
+        )
+
+    def settle(since):
+        for d in sends[since:]:
+            d.wait_send()
+        del sends[since:]
+
+    def send(src, dst, sem, flips):
+        d = copy(src, dst, sem, flips)
+        d.start()
+        sends.append(d)
+
+    def wait(ref, sem, flips):
+        copy(ref, ref, sem, flips).wait_recv()
+
+    class Gather:
+        def __init__(self, order, block):
+            self.order, self.block, self.sem = order, block, {}
+            for n in range(1, len(order) + 1):
+                for k in itertools.combinations(order, n):
+                    self.sem[frozenset(k)] = ids()
+
+        def push(self, *have):
+            have = frozenset(have)
+            last = max([self.order.index(d) for d in have], default=-1)
+            for d in self.order[last + 1 :]:
+                ref = self.block(at(have))
+                send(ref, ref, self.sem[have | {d}], (d,))
+
+        def pull(self, *have):
+            have = frozenset(have)
+            last = max(have, key=self.order.index)
+            wait(self.block(at(have)), self.sem[have], (last,))
+
+        def pass_on(self, *have):
+            self.pull(*have)
+            self.push(*have)
+
+    barrier = pltpu.get_barrier_semaphore()
+
+    def peer(j):
+        b = (me + j) % 32
+        return {"seq": b // 16, "ctx": (b // 2) % 8, "fsdp": b % 2}
+
+    loop(31, lambda j: pl.semaphore_signal(barrier, inc=1, device_id=peer(j + 1), device_id_type=MESH))
+
+    X16[s, h, l, y] = tok[...]
+    for k in range(HEADS):
+        parts = [qkvw[:, j * width + k * HEAD_DIM : j * width + (k + 1) * HEAD_DIM] for j in range(3)]
+        WP[k, :, 0 : 3 * HEAD_DIM] = jnp.concatenate(parts, axis=1)
+    WH[me] = WP[head]
+    G[me] = pack[...]
+    OW[h, y, x] = outw[...]
+    DW[h, y, x] = downw[...]
+
+    def quarter(sp, hp, lp):
+        return pl.ds(pl.multiple_of(sp * 2048 + hp * 1024 + lp * 512, 512), 512)
+
+    for hp in range(2):
+        UW[s, h, l, y, x, :, hp * 512 : (hp + 1) * 512] = upw[:, quarter(s, hp, l)]
+
+    pl.semaphore_wait(barrier, 31)
+
+    half = width // 2
+
+    def token_block(k):
+        return lambda p: X16.at[p["s"], p["h"], p["l"], p["y"], :, pl.ds(k * half, half)]
+
+    xg = [Gather("hyls", token_block(0)), Gather("hlys", token_block(1))]
+    for g in xg:
+        g.push()
+
+    def small_copy(j, dst):
+        b = (me + j) % 32
+        return [
+            pltpu.make_async_remote_copy(
+                src_ref=WP.at[b // 2], dst_ref=WH.at[dst], send_sem=wss.at[j], recv_sem=wrs.at[j],
+                device_id=peer(j), device_id_type=MESH),
+            pltpu.make_async_remote_copy(
+                src_ref=pack, dst_ref=G.at[dst], send_sem=gss.at[j], recv_sem=grs.at[j],
+                device_id=peer(j), device_id_type=MESH),
+        ]
+
+    loop(31, lambda j: [d.start() for d in small_copy(j + 1, me)])
+
+    up_sem = {}
+    for flips in (("s",), ("l",), ("s", "l")):
+        p = at(flips)
+        for hp in range(2):
+            up_sem[flips, hp] = ids()
+            send(
+                upw.at[:, quarter(p["s"], hp, p["l"])],
+                UW.at[s, h, l, y, x, :, pl.ds(hp * 512, 512)],
+                up_sem[flips, hp], flips,
+            )
+    og = Gather("hyx", lambda p: OW.at[p["h"], p["y"], p["x"]])
+    ug = Gather("hyx", lambda p: UW.at[:, p["h"], :, p["y"], p["x"]])
+    dg = Gather("hyx", lambda p: DW.at[p["h"], p["y"], p["x"]])
+    og.push()
+
+    for g, a, b in ((xg[0], "y", "l"), (xg[1], "l", "y")):
+        g.pass_on("h")
+    for flips in (("s",), ("l",), ("s", "l")):
+        p = at(flips)
+        for hp in range(2):
+            wait(UW.at[p["s"], h, p["l"], y, x, :, pl.ds(hp * 512, 512)], up_sem[flips, hp], flips)
+    ug.push()
+    xg[0].pass_on("y")
+    xg[1].pass_on("l")
+    xg[0].pass_on("h", "y")
+    xg[1].pass_on("h", "l")
+    og.pass_on("h")
+    og.pass_on("y")
+    og.pass_on("h", "y")
+    dg.push()
+    for have in (("l",), ("h", "l"), ("y", "l"), ("h", "y", "l")):
+        xg[0].pass_on(*have)
+    for have in (("y",), ("h", "y"), ("l", "y"), ("h", "l", "y")):
+        xg[1].pass_on(*have)
+    ug.pass_on("h")
+    ug.pass_on("y")
+    ug.pass_on("h", "y")
+
+    def wait_small(j):
+        for d in small_copy(j + 1, (me + 31 - j) % 32):
+            d.wait_recv()
+
+    loop(31, wait_small)
+
+    spread = [spread_matrix(width, 32, j).astype(BF16) for j in range(4)]
+    mine = own_columns(32, width)
+    for row, j, to in ((0, 2, 0), (0, 3, 1), (1, 0, 2), (1, 1, 3), (1, 2, 4), (1, 3, 5)):
+        rows = G[:, row, :].astype(BF16)
+        VEC[to : to + 1, :] = jnp.sum(jnp.where(mine, dot(rows, spread[j]), 0.0), axis=0, keepdims=True)
+    for hp, yp, xp in itertools.product(range(2), repeat=3):
+        r = hp * 4 + yp * 2 + xp
+        UB[0:1, r * 128 : (r + 1) * 128] = G[s * 16 + hp * 8 + l * 4 + yp * 2 + xp, 2:3, :]
+    out_bias, down_bias = VEC[0:1, :], VEC[1:2, :]
+    gain_one, shift_one, gain_two, shift_two = (VEC[k : k + 1, :] for k in range(2, 6))
+    first, second = G[head * 2, 0:1, :], G[head * 2 + 1, 0:1, :]
+    head_bias = jnp.concatenate(
+        [first[:, 0:32], second[:, 0:32], jnp.zeros((1, 64), F32), first[:, 32:64], second[:, 32:64]], axis=1
+    )
+    head_weight = WH[...].reshape(width, WH.shape[2])[:, 0 : 3 * HEAD_DIM]
+
+    length = 8 * tok.shape[0]
+    qtiles = length // TILE
+    scale = HEAD_DIM ** (-0.5)
+    DH4, DB4, DSUM = C4, N4, FN
+
+    def project(j):
+        sp = s if j == 0 else 1 - s
+
+        def body(i):
+            hl = X16[sp, i // 2, i % 2].reshape(TILE, width)
+            res = (dot(hl, head_weight) + head_bias).astype(BF16).astype(F32)
+            rows = pl.ds(pl.multiple_of(i * TILE, TILE), TILE)
+            QN[j, rows, :] = res[:, 0:64].astype(BF16)
+            KN[j, rows, :] = res[:, 64:128].astype(BF16)
+            VN[j, rows, :] = res[:, 128:192].astype(BF16)
+            QKVT[j, :, rows] = res.T.astype(BF16)
+
+        loop(qtiles, body)
+
+    def attend(j):
+        def body(i):
+            cols = pl.ds(pl.multiple_of(i * TILE, TILE), TILE)
+            q = QKVT[j, 0:64, cols] * jnp.asarray(scale, BF16)
+            st = dot(KN[j], q)
+            top = jnp.max(st, axis=0, keepdims=True)
+            e = jnp.exp(st - top)
+            total = jnp.sum(e, axis=0, keepdims=True)
+            o = dot(QKVT[j, 128:192, :], e.astype(BF16)) / total
+            OT[j, :, cols] = o
+            OTB[j, :, cols] = o.astype(BF16)
+            LSE[j, 0:1, cols] = top + jnp.log(total)
+
+        loop(qtiles, body)
+
+    project(0)
+    attend(0)
+    for have in (("s",), ("h", "s"), ("y", "s"), ("h", "y", "s"), ("l", "s"), ("h", "l", "s"), ("y", "l", "s"), ("h", "y", "l", "s")):
+        for g in xg:
+            g.pull(*have)
+    project(1)
+    attend(1)
+    dg.pass_on("h")
+    dg.pass_on("y")
+    dg.pass_on("h", "y")
+
+    tokens = tok.shape[0]
+
+    def tok_cols(hp, lp, yp):
+        return pl.ds(pl.multiple_of((hp * 4 + lp * 2 + yp) * tokens, tokens), tokens)
+
+    others = (("h",), ("y",), ("h", "y"))
+    a_sem = {f: ids() for f in others}
+    for k, flips in enumerate(((),) + others):
+        p = at(flips)
+        for sp, lp in itertools.product(range(2), repeat=2):
+            j = s if sp == 0 else 1 - s
+            to = pl.ds((sp * 2 + lp) * tokens, tokens)
+            piece = OTB[j, :, tok_cols(p["h"], lp, p["y"])]
+            if flips:
+                AS[k, :, to] = piece
+            else:
+                AT[h, y, :, to] = piece
+        if flips:
+            send(AS.at[k], AT.at[h, y], a_sem[flips], flips)
+    for have in (("x",), ("h", "x"), ("y", "x"), ("h", "y", "x")):
+        og.pull(*have)
+    for flips in others:
+        p = at(flips)
+        wait(AT.at[p["h"], p["y"]], a_sem[flips], flips)
+
+    group = 4 * tokens
+    A4[...] = AT[...].reshape(4 * HEAD_DIM, group).astype(F32).T.astype(BF16)
+
+    def group_sum(bufs, tile_fn):
+        sa, ra, sb, rb = bufs
+        base_a, base_b = [ids() for _ in range(tiles)][0], [ids() for _ in range(tiles)][0]
+
+        def a(i):
+            sa[i] = tile_fn(1 - s, i).astype(BF16)
+            copy(sa.at[i], ra.at[i], base_a + i, ("s",)).start()
+
+        loop(tiles, a)
+
+        def b(i):
+            v = tile_fn(s, i)
+            wait(ra.at[i], base_a + i, ("s",))
+            KR[i] = (v + ra[i].astype(F32)).reshape(2, tokens, TILE)
+            sb[i] = KR[i, 1 - l].astype(BF16)
+            copy(sb.at[i], rb.at[i], base_b + i, ("l",)).start()
+
+        loop(tiles, b)
+        for i in range(tiles):
+            wait(rb.at[i], base_b + i, ("l",))
+        for i in range(tiles):
+            sends.append(copy(sa.at[i], ra.at[i], base_a + i, ("s",)))
+            sends.append(copy(sb.at[i], rb.at[i], base_b + i, ("l",)))
+        return jnp.concatenate([KR[i, l] + rb[i].astype(F32) for i in range(tiles)], axis=1)
+
+    def group_rows(sp):
+        return pl.ds(pl.multiple_of(sp * 2 * tokens, 2 * tokens), 2 * tokens)
+
+    def col_tile(i):
+        return pl.ds(pl.multiple_of(i * TILE, TILE), TILE)
+
+    mark = len(sends)
+    branch = group_sum(
+        (R1A, R1B, R1C, R1D),
+        lambda sp, i: dot(A4[group_rows(sp), :], OW[:, :, :, :, col_tile(i)].reshape(4 * HEAD_DIM, TILE)),
+    )
+
+    def norm_forward(values, gain, shift):
+        centered = values - jnp.mean(values, axis=-1, keepdims=True)
+        recip = lax.rsqrt(jnp.mean(centered * centered, axis=-1, keepdims=True) + epsilon)
+        normal = centered * recip
+        return normal * gain + shift, normal, recip
+
+    def norm_backward(upstream, normal, recip, gain):
+        gain_grad = jnp.sum(upstream * normal, axis=0, keepdims=True)
+        shift_grad = jnp.sum(upstream, axis=0, keepdims=True)
+        scaled = upstream * gain
+        inner = (
+            scaled
+            - jnp.mean(scaled, axis=-1, keepdims=True)
+            - normal * jnp.mean(scaled * normal, axis=-1, keepdims=True)
+        )
+        return recip * inner, gain_grad, shift_grad
+
+    first_norm, normal_one, recip_one = norm_forward(
+        tok[...].astype(F32) + branch + out_bias, gain_one, shift_one
+    )
+    FN[...] = first_norm
+    NORM1[...] = normal_one
+
+    def group_gather(ref, value, meanwhile=None):
+        g = Gather("ls", lambda p: ref.at[p["s"], p["l"]])
+        ref[s, l] = value
+        g.push()
+        if meanwhile is not None:
+            meanwhile()
+        g.pass_on("l")
+        g.pull("s")
+        g.pull("l", "s")
+
+    group_gather(N4, first_norm.astype(BF16))
+    settle(mark)
+
+    for have in (("x",), ("h", "x"), ("y", "x"), ("h", "y", "x")):
+        ug.pull(*have)
+    hidden = UB.shape[1]
+
+    def all_rows(ref):
+        return ref[...].reshape(group, ref.shape[-1])
+
+    def up(i):
+        cols = col_tile(i)
+        w = UW[:, :, :, :, :, :, cols].reshape(width, TILE)
+        pre = dot(all_rows(N4), w) + UB[0:1, cols]
+        phi = 0.5 * (1.0 + lax.erf(pre * (2.0 ** -0.5)))
+        act = pre * phi
+        GP[:, cols] = phi + pre * (jnp.exp(-0.5 * pre * pre) * ((2.0 * math.pi) ** -0.5))
+        C4[:, cols] = act.astype(BF16)
+
+    loop(hidden // TILE, up)
+    for have in (("x",), ("h", "x"), ("y", "x"), ("h", "y", "x")):
+        dg.pull(*have)
+    feed = group_sum(
+        (R2A, R2B, R2C, R2D),
+        lambda sp, i: dot(C4[group_rows(sp), :], DW[:, :, :, :, col_tile(i)].reshape(hidden, TILE)),
+    )
+    final, normal_two, recip_two = norm_forward(FN[...] + feed + down_bias, gain_two, shift_two)
+    out_o[...] = final.astype(BF16)
+    d_second, gain_two_grad, shift_two_grad = norm_backward(
+        cot[...].astype(F32), normal_two, recip_two, gain_two
+    )
+    DSEC[...] = d_second
+    d_feed = d_second.astype(BF16)
+    VG[1:2, :] = jnp.sum(d_feed.astype(F32), axis=0, keepdims=True)
+    VG[4:5, :] = gain_two_grad
+    VG[5:6, :] = shift_two_grad
+
+    def transpose_rows(i):
+        cols = pl.ds(pl.multiple_of(i * 128, 128), 128)
+        t = N4[:, :, :, cols].reshape(group, 128)
+        t = t.astype(F32).T.astype(BF16).reshape(2, 2, 32, group)
+        for yp, xp in itertools.product(range(2), repeat=2):
+            to = pl.ds(pl.multiple_of((i // 4 * 2 + i % 2) * 32, 32), 32)
+            N4T[(i // 2) % 2, yp, xp, to, :] = t[yp, xp]
+        C4T[i // 4, (i // 2) % 2, i % 2] = C4[:, cols].astype(F32).T.astype(BF16)
+
+    group_gather(DF4, d_feed, lambda: loop(8, transpose_rows))
+
+    def d_hidden(i):
+        rows = DW[i // 2, i % 2].reshape(TILE, width)
+        cols = col_tile(i)
+        v = (dot(all_rows(DF4), rows, 1, 1) * GP[:, cols]).astype(BF16)
+        DH4[:, cols] = v
+        UB[1:2, cols] = jnp.sum(v.astype(F32), axis=0, keepdims=True)
+
+    loop(hidden // TILE, d_hidden)
+
+    def up_rows(i):
+        return UW[i // 2, i % 2].reshape(TILE, hidden)
+
+    d_first = group_sum(
+        (R1A, R1B, R1C, R1D), lambda sp, i: dot(DH4[group_rows(sp), :], up_rows(i), 1, 1)
+    )
+    d_sum_one, gain_one_grad, shift_one_grad = norm_backward(
+        DSEC[...] + d_first, NORM1[...], recip_one, gain_one
+    )
+    DSUM[...] = d_sum_one
+    d_branch = d_sum_one.astype(BF16)
+    VG[0:1, :] = jnp.sum(d_branch.astype(F32), axis=0, keepdims=True)
+    VG[2:3, :] = gain_one_grad
+    VG[3:4, :] = shift_one_grad
+    group_gather(DB4, d_branch)
+
+    d_att = dot(all_rows(DB4), OW[...].reshape(4 * HEAD_DIM, width), 1, 1).astype(BF16)
+    d_att = d_att.astype(F32).T.astype(BF16).reshape(2, 2, HEAD_DIM, group)
+    DS[...] = d_att
+    d_sem = {f: ids() for f in others}
+    for flips in others:
+        p = at(flips)
+        send(DS.at[p["h"], p["y"]], DR.at[h, y], d_sem[flips], flips)
+    DR[h, y] = DS[h, y]
+
+    class Scatter:
+        def __init__(self, bufs, product):
+            self.sa, self.ra, self.sb, self.rb, self.sc, self.rc, self.keep = bufs
+            self.product = product
+            self.a, self.b, self.c = ([ids() for _ in range(tiles)][0] for _ in range(3))
+            self.shape = self.sa.shape[1:]
+
+        def done(self, src, dst, base, dim):
+            for i in range(tiles):
+                sends.append(copy(src.at[i], dst.at[i], base + i, (dim,)))
+
+        def first(self):
+            def body(i):
+                self.sa[i] = self.product(1 - x, i).reshape(self.shape).astype(BF16)
+                copy(self.sa.at[i], self.ra.at[i], self.a + i, ("x",)).start()
+
+            loop(tiles, body)
+            self.done(self.sa, self.ra, self.a, "x")
+
+        def second(self):
+            def body(i):
+                v = self.product(x, i).reshape(self.shape)
+                wait(self.ra.at[i], self.a + i, ("x",))
+                self.keep[i] = v + self.ra[i].astype(F32)
+                self.sb[i] = self.keep[i, :, 1 - y].astype(BF16)
+                copy(self.sb.at[i], self.rb.at[i], self.b + i, ("y",)).start()
+
+            loop(tiles, body)
+            self.done(self.sb, self.rb, self.b, "y")
+
+        def third(self):
+            def body(i):
+                wait(self.rb.at[i], self.b + i, ("y",))
+                self.keep[i, :, 0] = self.keep[i, :, y] + self.rb[i].astype(F32)
+                self.sc[i] = self.keep[i, 1 - h, 0].astype(BF16)
+                copy(self.sc.at[i], self.rc.at[i], self.c + i, ("h",)).start()
+
+            loop(tiles, body)
+            self.done(self.sc, self.rc, self.c, "h")
+
+        def last(self, out):
+            def body(i):
+                wait(self.rc.at[i], self.c + i, ("h",))
+                out[:, col_tile(i)] = self.keep[i, h, 0] + self.rc[i].astype(F32)
+
+            loop(tiles, body)
+
+    def up_product(xp, i):
+        return dot(N4T[:, :, xp].reshape(group, group), DH4[:, col_tile(i)])
+
+    def down_product(xp, i):
+        return dot(
+            C4T[:, :, xp].reshape(group, group),
+            DF4[:, :, :, col_tile(i)].reshape(group, TILE),
+        )
+
+    def out_product(xp, i):
+        rows = pl.ds(pl.multiple_of(xp * 32, 32), 32)
+        return dot(
+            AT[:, :, rows, :].reshape(128, group),
+            DB4[:, :, :, col_tile(i)].reshape(group, TILE),
+        )
+
+    down_s = Scatter((DSA, DRA, DSB, DRB, DSC, DRC, DK), down_product)
+    up_s = Scatter((USA, URA, USB, URB, USC, URC, UK), up_product)
+    out_s = Scatter((OSA, ORA, OSB, ORB, OSC, ORC, OK), out_product)
+    down_s.first()
+    up_s.first()
+    out_s.first()
+
+    for flips in others:
+        p = at(flips)
+        wait(DR.at[p["h"], p["y"]], d_sem[flips], flips)
+    for sp in range(2):
+        j = s if sp == 0 else 1 - s
+        for hp, lp, yp in itertools.product(range(2), repeat=3):
+            part = DR[hp, yp, :, (sp * 2 + lp) * tokens : (sp * 2 + lp + 1) * tokens]
+            at_tok = (hp * 4 + lp * 2 + yp) * tokens
+            DAT[j, :, at_tok : at_tok + tokens] = part
+            DA[j, at_tok : at_tok + tokens, :] = part.astype(F32).T.astype(BF16)
+
+    def attend_back(j):
+        DKV[...] = jnp.zeros_like(DKV)
+
+        def body(i):
+            cols = col_tile(i)
+            q = QKVT[j, 0:64, cols] * jnp.asarray(scale, BF16)
+            p = jnp.exp(dot(KN[j], q) - LSE[j, 0:1, cols])
+            da = DAT[j, :, cols]
+            delta = jnp.sum(da.astype(F32) * OT[j, :, cols], axis=0, keepdims=True)
+            dp = dot(VN[j], da)
+            ds = (p * (dp - delta) * scale).astype(BF16)
+            DQT[j, :, cols] = dot(QKVT[j, 64:128, :], ds)
+            DKV[0] += dot(ds, QN[j, cols, :])
+            DKV[1] += dot(p.astype(BF16), DA[j, cols, :])
+
+        loop(qtiles, body)
+        dqt = DQT[j].astype(BF16).astype(F32)
+        dq = dqt.T
+        dk, dv = DKV[0].astype(BF16).astype(F32), DKV[1].astype(BF16).astype(F32)
+        DQKV[j] = jnp.concatenate([dq, dk, dv], axis=1).astype(BF16)
+        DQKVT[j, 0:64, :] = dqt.astype(BF16)
+        DQKVT[j, 64:128, :] = dk.T.astype(BF16)
+        DQKVT[j, 128:192, :] = dv.T.astype(BF16)
+        return jnp.sum(dq, axis=0, keepdims=True), jnp.sum(dv, axis=0, keepdims=True)
+
+    q0, v0 = attend_back(0)
+    down_s.second()
+    q1, v1 = attend_back(1)
+    up_s.second()
+    out_s.second()
+    down_s.third()
+    up_s.third()
+
+    def input_tile(j, i):
+        w = WH[pl.ds(pl.multiple_of(i * 8, 8), 8)].reshape(TILE, WH.shape[2])[:, 0 : 3 * HEAD_DIM]
+        return dot(DQKV[j], w, 1, 1).reshape(2, 2, 2, tokens, TILE)
+
+    ia, ib, ic, id_ = ([ids() for _ in range(tiles)][0] for _ in range(4))
+
+    def in_sent(i):
+        return (C4T if i < tiles // 2 else N4T).at[:, :, :, :, pl.ds(i % 2 * TILE, TILE)]
+
+    for i in range(tiles):
+        in_sent(i)[...] = input_tile(1, i).astype(BF16)
+        send(in_sent(i), IRA.at[i], ia + i, ("s",))
+
+    qa = [ids() for _ in range(tiles)][0]
+
+    def q_first(i):
+        cols = col_tile(i)
+        v = dot(DQKVT[0], X16[s, :, :, :, :, cols].reshape(length, TILE))
+        v += dot(DQKVT[1], X16[1 - s, :, :, :, :, cols].reshape(length, TILE))
+        v = v.T.reshape(2, 2, 2, 32, 3 * HEAD_DIM)
+        for xp in range(2):
+            QK[i, xp] = v[:, :, xp]
+        QSA[i, :, :, :, 0 : 3 * HEAD_DIM] = QK[i, 1 - x].astype(BF16)
+        copy(QSA.at[i], QRA.at[i], qa + i, ("x",)).start()
+
+    for i in range(tiles):
+        dims = ("l", "y") if i < tiles // 2 else ("y", "l")
+        wait(IRA.at[i], ia + i, ("s",))
+        IK[i] = input_tile(0, i) + IRA[i].astype(F32)
+        ISB[i] = (IK[i, :, 1 - l] if dims[0] == "l" else IK[i, :, :, 1 - y]).astype(BF16)
+        send(ISB.at[i], IRB.at[i], ib + i, (dims[0],))
+    loop(tiles, q_first)
+    out_s.third()
+
+    bq, bv = q0 + q1, v0 + v1
+    VG[6:8, :] = jnp.zeros((2, width), F32)
+    picked = [spread_matrix(width, 32, j) for j in range(4)]
+
+    def exact_pick(row, j):
+        a = jnp.where(mine, VG[row : row + 1, :], 0.0)
+        hi = a.astype(BF16)
+        rest = a - hi.astype(F32)
+        mid = rest.astype(BF16)
+        low = (rest - mid.astype(F32)).astype(BF16)
+        r = picked[j].astype(BF16)
+        return dot(hi, r, 1, 1) + dot(mid, r, 1, 1) + dot(low, r, 1, 1)
+
+    SG[...] = jnp.zeros_like(SG)
+    SG[:, 0, :] = exact_pick(0, 2) + exact_pick(1, 3)
+    SG[:, 1, :] = exact_pick(2, 0) + exact_pick(3, 1) + exact_pick(4, 2) + exact_pick(5, 3)
+    for k in range(2):
+        b = head * 2 + k
+        lanes = slice(k * 32, k * 32 + 32)
+        SG[b, 0:1, :] += jnp.concatenate([bq[:, lanes], bv[:, lanes], jnp.zeros((1, 64), F32)], axis=1)
+    for hp, yp, xp in itertools.product(range(2), repeat=3):
+        r = hp * 4 + yp * 2 + xp
+        SG[s * 16 + hp * 8 + l * 4 + yp * 2 + xp, 2:3, :] = UB[1:2, r * 128 : (r + 1) * 128]
+
+    def grad_copy(j):
+        b = (me + j) % 32
+        return pltpu.make_async_remote_copy(
+            src_ref=SG.at[b], dst_ref=RG.at[j], send_sem=hss.at[j], recv_sem=hrs.at[j],
+            device_id=peer(j), device_id_type=MESH)
+
+    loop(31, lambda j: grad_copy(j + 1).start())
+    RG[0] = SG[me]
+
+    for i in range(tiles):
+        dims = ("l", "y") if i < tiles // 2 else ("y", "l")
+        wait(IRB.at[i], ib + i, (dims[0],))
+        if dims[0] == "l":
+            u = IK[i, :, l] + IRB[i].astype(F32)
+            IK[i, :, 0] = u
+            ISC[i] = IK[i, :, 0, 1 - y].astype(BF16)
+        else:
+            u = IK[i, :, :, y] + IRB[i].astype(F32)
+            IK[i, :, 0] = u
+            ISC[i] = IK[i, :, 0, 1 - l].astype(BF16)
+        send(ISC.at[i], IRC.at[i], ic + i, (dims[1],))
+
+    def q_second(i):
+        wait(QRA.at[i], qa + i, ("x",))
+        v = QK[i, x] + QRA[i, :, :, :, 0 : 3 * HEAD_DIM].astype(F32)
+        QSB[i // 2, i % 2, :, :, :, 0 : 3 * HEAD_DIM] = v.astype(BF16)
+
+    loop(tiles, q_second)
+    for i in range(tiles):
+        sends.append(copy(QSA.at[i], QRA.at[i], qa + i, ("x",)))
+
+    def piece_copy(j):
+        to = (head + j) % 16
+        return pltpu.make_async_remote_copy(
+            src_ref=QSB.at[to // 8, (to // 4) % 2, (to // 2) % 2, to % 2], dst_ref=QG.at[head],
+            send_sem=hss.at[32 + j], recv_sem=hrs.at[32 + j],
+            device_id={"seq": to // 8, "ctx": to % 8, "fsdp": x}, device_id_type=MESH)
+
+    loop(15, lambda j: piece_copy(j + 1).start())
+    QG[head] = QSB[s, h, l, y]
+
+    down_s.last(downg_o)
+    up_s.last(UF)
+    uf_sem = {}
+    for flips in (("s",), ("l",), ("s", "l")):
+        p = at(flips)
+        for hp in range(2):
+            uf_sem[flips, hp] = ids()
+            send(
+                UF.at[pl.ds(pl.multiple_of((p["s"] * 2 + p["l"]) * 32, 32), 32), pl.ds(hp * 512, 512)],
+                upg_o.at[:, quarter(s, hp, l)], uf_sem[flips, hp], flips,
+            )
+    for hp in range(2):
+        upg_o[:, quarter(s, hp, l)] = UF[pl.ds(pl.multiple_of((s * 2 + l) * 32, 32), 32), hp * 512 : (hp + 1) * 512]
+
+    for i in range(tiles):
+        dims = ("l", "y") if i < tiles // 2 else ("y", "l")
+        wait(IRC.at[i], ic + i, (dims[1],))
+        mine_at = y if dims[0] == "l" else l
+        IK[i, :, 1, 0] = IK[i, :, 0, mine_at] + IRC[i].astype(F32)
+        ISD[i] = IK[i, 1 - h, 1, 0].astype(BF16)
+        send(ISD.at[i], IRD.at[i], id_ + i, ("h",))
+    out_s.last(outg_o)
+
+    loop(31, lambda j: grad_copy(j + 1).wait_recv())
+    small_o[...] = jnp.sum(RG[...], axis=0)
+
+    loop(15, lambda j: piece_copy(j + 1).wait_recv())
+    for k in range(HEADS // 2):
+        a, b = QG[2 * k].astype(F32), QG[2 * k + 1].astype(F32)
+        for part in range(3):
+            lanes = slice(part * 64, part * 64 + 64)
+            to = part * width + k * 128
+            qkvg_o[:, to : to + 128] = jnp.concatenate([a[:, lanes], b[:, lanes]], axis=1)
+
+    for i in range(tiles):
+        wait(IRD.at[i], id_ + i, ("h",))
+        cols = slice(i * TILE, (i + 1) * TILE)
+        ig_o[:, cols] = IK[i, h, 1, 0] + IRD[i].astype(F32) + DSUM[:, cols]
+
+    for flips in (("s",), ("l",), ("s", "l")):
+        p = at(flips)
+        for hp in range(2):
+            wait(upg_o.at[:, quarter(p["s"], hp, p["l"])], uf_sem[flips, hp], flips)
+
+    for d in sends:
+        d.wait_send()
+
+    def small_sent(j):
+        for d in small_copy(j + 1, me):
+            d.wait_send()
+        grad_copy(j + 1).wait_send()
+
+    loop(31, small_sent)
+    loop(15, lambda j: piece_copy(j + 1).wait_send())
+
+
+def on_block(
+    tokens, qkv_weight, out_weight, up_weight, down_weight,
+    query_bias, value_bias, out_bias, up_bias, down_bias,
+    norm1_gain, norm1_bias, norm2_gain, norm2_bias, cotangent,
+):
+    n, width = tokens.shape[1], tokens.shape[2]
+    hidden = up_weight.shape[1] // 4
+    group = 4 * n
+    length = 8 * n
+    tiles = width // TILE
+    small = jnp.concatenate(
+        [query_bias, value_bias, out_bias, down_bias, norm1_gain, norm1_bias, norm2_gain, norm2_bias, up_bias]
+    ).astype(F32).reshape(3, 128)
+    pack = jnp.pad(small, ((0, 5), (0, 0)))
+
+    def b(*shape):
+        return pltpu.VMEM(shape, BF16)
+
+    def f(*shape):
+        return pltpu.VMEM(shape, F32)
+
+    group_bufs = [b(tiles, 2 * n, TILE), b(tiles, 2 * n, TILE), b(tiles, n, TILE), b(tiles, n, TILE)]
+
+    def scatter_bufs(rows):
+        return [
+            b(tiles, 2, 2, rows, TILE), b(tiles, 2, 2, rows, TILE),
+            b(tiles, 2, rows, TILE), b(tiles, 2, rows, TILE),
+            b(tiles, rows, TILE), b(tiles, rows, TILE),
+            f(tiles, 2, 2, rows, TILE),
+        ]
+
+    sem = pltpu.SemaphoreType.DMA
+    scratch = [
+        b(2, 2, 2, 2, n, width), b(HEADS, 32, 256), b(32, 32, 256), f(32, 8, 128),
+        b(2, 2, 2, 32, width), b(2, 2, 2, 2, 2, 32, hidden), b(2, 2, 2, 128, width),
+        b(2, length, 64), b(2, length, 64), b(2, length, 64), b(2, 192, length), f(2, 64, length), b(2, 64, length),
+        f(2, 8, length), b(4, 64, group), b(2, 2, 64, group), b(group, 256),
+        *group_bufs, *group_bufs, f(tiles, 2, n, TILE),
+        b(2, 2, n, width), b(2, 2, 2, 128, group), b(group, hidden), b(2, 2, 2, 128, group), f(group, hidden),
+        b(2, 2, n, width),
+        f(n, width), f(n, width), f(n, width),
+        b(2, 2, 64, group), b(2, 2, 64, group), b(2, length, 64), b(2, 64, length), f(2, length, 64), f(2, 64, length),
+        b(2, length, 192), b(2, 192, length),
+        *scatter_bufs(128), f(128, width),
+        *scatter_bufs(128),
+        *scatter_bufs(32),
+        b(tiles, 2, 2, 2, n, TILE), b(tiles, 2, 2, n, TILE), b(tiles, 2, 2, n, TILE),
+        b(tiles, 2, n, TILE), b(tiles, 2, n, TILE), b(tiles, n, TILE), b(tiles, n, TILE), f(tiles, 2, 2, 2, n, TILE),
+        b(tiles, 2, 2, 32, 256), b(tiles, 2, 2, 32, 256), f(tiles, 2, 2, 2, 32, 192), b(2, 2, 2, 2, 32, 256), b(HEADS, 32, 256),
+        f(8, width), f(8, hidden), f(8, width), f(32, 8, 128), f(32, 8, 128),
+        sem((256,)), sem((256,)), sem((32,)), sem((32,)), sem((32,)), sem((32,)), sem((48,)), sem((48,)),
+    ]
+    vmem = pl.BlockSpec(memory_space=pltpu.VMEM)
+    shapes = [
+        jax.ShapeDtypeStruct((n, width), BF16),
+        jax.ShapeDtypeStruct((n, width), F32),
+        jax.ShapeDtypeStruct((32, 3 * width), F32),
+        jax.ShapeDtypeStruct((32, width), F32),
+        jax.ShapeDtypeStruct((32, 4 * hidden), F32),
+        jax.ShapeDtypeStruct((128, width), F32),
+        jax.ShapeDtypeStruct((8, 128), F32),
+    ]
+    out, ig, qkvg, outg, upg, downg, sm = pl.pallas_call(
+        layer_kernel,
+        out_shape=shapes,
+        in_specs=[vmem] * 7,
+        out_specs=[vmem] * 7,
+        scratch_shapes=scratch,
+        compiler_params=pltpu.CompilerParams(
+            collective_id=0, has_side_effects=True, vmem_limit_bytes=63 * 2**20
+        ),
+        name="layer",
+    )(tokens[0], qkv_weight, out_weight, up_weight, down_weight, pack, cotangent[0])
+    row0, row1 = sm[0], sm[1]
+    return (
+        out[None], ig[None], qkvg, outg, upg, downg,
+        row0[0:32], row0[32:64], row0[64:96], sm[2], row0[96:128],
+        row1[0:32], row1[32:64], row1[64:96], row1[96:128],
+    )
+
+
 def solution(mesh):
     placed = (
         P(("seq", "fsdp"), "ctx", None),
@@ -256,8 +1053,9 @@
         P(("seq", "ctx", "fsdp")),
         P(("seq", "fsdp"), "ctx", None),
     )
+    fast = dict(mesh.shape) == {"seq": 2, "ctx": 8, "fsdp": 2}
     return jax.shard_map(
-        on_device,
+        on_block if fast else on_device,
         mesh=mesh,
         in_specs=placed,
         out_specs=(

time: 1650 us -> 270 us (0.16)
  waiting for transfers between devices: 1320 us -> 0 us
  Pallas kernels: 0 us -> 254 us
  blocking collectives: 150 us -> 0 us
  matrix products: 81.6 us -> 0 us
  local copies, waits for them, and re-layouts: 73.1 us -> 14 us
    reduce_scatter x4 -> x0, waiting for transfers between devices: 920 us -> none  [the longest x1 363 us: on_device(): lax.psum_scatter(up_grad, ('seq', 'ctx', 'fsdp'), scatter_dimension=0, ti...]
    pallas_call x0 -> x1, Pallas kernels: none -> 254 us  [on_block(): pl.pallas_call(layer_kernel, out_shape=shapes, in_specs=[vmem] * 7, out_s...]
    all_gather x6 -> x0, waiting for transfers between devices: 233 us -> none  [the longest x1 76 us: on_device(): lax.all_gather(up_weight, ('seq', 'ctx', 'fsdp'), axis=0, tiled=True)]
    unnamed x12 -> x0, waiting for transfers between devices: 162 us -> none
    unnamed x2 -> x0, blocking collectives: 83.9 us -> none
    dot_general x26 -> x0, matrix products: 81.6 us -> none  [the longest x12 68.2 us: matmul(): jnp.dot(left_neighbor, right_neighbor, preferred_element_type=jnp.float32)]
    all_gather x1 -> x0, blocking collectives: 65.6 us -> none  [on_device(): lax.all_gather(up_bias, ('seq', 'ctx', 'fsdp'), axis=0, tiled=True)]
    unnamed x70 -> x22, local copies, waits for them, and re-layouts: 40.6 us -> 7.2 us
  transfers between devices with their start and end apart: 11 -> 0, of which waited for: 10 -> 0; matrix products, arithmetic and copies ran while one was open for 6% -> 0% of each run, Pallas kernels for 0% -> 0%
where the time goes in v1:
time: 270 us
  Pallas kernels  254 us (94%)
  local copies, waits for them, and re-layouts  14 us (5%)
    pallas_call x1, Pallas kernels, on_block(): pl.pallas_call(layer_kernel, out_shape=shapes, in_specs=[vmem] * 7, out_s...  254 us
    unnamed x22, local copies, waits for them, and re-layouts  7.2 us

profile of v1, /device:TPU:1, one launch (start us, length us, event | category | flops | bytes accessed | tf_op | source)
XLA Modules:
  0.0 269.7 jit_solution(13566505961261248122)
XLA Ops:
  0.6 0.0 copy-start.5
  0.7 0.0 copy-start.6
  0.7 0.0 copy-start.7
  0.7 0.6 copy-done.5
  1.3 0.0 copy-done.6
  1.3 0.0 copy-done.7
  1.3 4.1 %concatenate.3 = bf16[384]{0:T(512)(128)(2,1)S(1)} concatenate(bf16[32]{0:T(256)(128)(2,1)S(1)} %copy-done.5, bf16[32]{0:T(256)(128)(2,1)S(1)} %copy-done.6, bf16[32]{0:T(256)(128)(2,1)S(1)} %copy-done.7, bf16[32]{0:T(256)(128)(2,1)} %param.24, bf16[32]{0:T(256)(128)(2,1)} %param.25, bf16[32]{0:T(256)(128)(2,1)} %param.26, bf16[32]{0:T(256)(128)(2,1)} %param.27, ...), dimensions={0} | concatenate | bytes 1536 | tf_op jit(solution)/shard_map/concatenate | solution.py:967
  5.4 0.6 pad_convert_fusion.pack
  6.0 254.3 %layer.1 = (bf16[128,1024]{1,0:T(8,128)(2,1)}, f32[128,1024]{1,0:T(8,128)}, f32[32,3072]{1,0:T(8,128)}, f32[32,1024]{1,0:T(8,128)}, f32[32,4096]{1,0:T(8,128)}, /*index=5*/f32[128,1024]{1,0:T(8,128)}, f32[8,128]{1,0:T(8,128)}) custom-call(bf16[128,1024]{1,0:T(8,128)(2,1)} %bitcast.24, bf16[32,3072]{1,0:T(8,128)(2,1)} %qkvw.1, bf16[32,1024]{1,0:T(8,128)(2,1)} %outw.1, ...), custom_call_target="tpu_custom_call" | custom-call | tf_op jit(solution)/shard_map/layer/pallas_call | solution.py:1019
  260.4 0.0 copy-start.2
  260.4 1.6 slice_bitcast_fusion
  261.9 1.2 slice_bitcast_fusion.5
  263.1 1.7 copy.36
  264.8 0.0 copy-done.2
  264.8 0.0 copy-start.3
  264.8 0.8 copy.37
  265.6 0.4 copy-done.3
  266.0 0.0 copy-start.4
  266.0 0.0 copy-start.1
  266.0 0.7 copy.38
  266.7 0.2 copy-done.4
  267.0 0.7 copy.39
  267.6 0.0 copy-done.1
  267.6 0.0 copy-start
  267.6 0.8 copy.40
  268.4 0.4 copy-done
  268.9 0.8 copy.41
Async XLA Ops:
  0.6 0.7 copy-start.5
  0.7 0.7 copy-start.6
  0.7 0.7 copy-start.7
  260.4 4.4 %copy-start.2 = (f32[128,1024]{1,0:T(8,128)S(1)}, f32[128,1024]{1,0:T(8,128)}, u32[]{:S(2)}) copy-start(f32[128,1024]{1,0:T(8,128)} %get-tuple-element.23) | copy-start | bytes 1572868
  264.8 1.2 copy-start.3
  266.0 1.0 copy-start.4
  266.0 1.7 copy-start.1
  267.6 1.2 copy-start

commit v2 on v1

--- a/solution.py
+++ b/solution.py
@@ -269,13 +269,13 @@
 def own_columns(blocks, width):
     row = lax.broadcasted_iota(jnp.int32, (blocks, width), 0)
     column = lax.broadcasted_iota(jnp.int32, (blocks, width), 1)
-    return column // (width // blocks) == row
+    return column // (width // blocks), row
 
 
 def layer_kernel(
-    tok, qkvw, outw, upw, downw, pack, cot,
+    tok, qkvw, outw, upw, downw, qb, vb, ob, ub, db, g1, b1, g2, b2, cot,
     out_o, ig_o, qkvg_o, outg_o, upg_o, downg_o, small_o,
-    X16, WP, WH, G, OW, UW, DW,
+    PK, X16, WP, WH, G, OW, UW, DW,
     QN, KN, VN, QKVT, OT, OTB, LSE, AS, AT, A4,
     R1A, R1B, R1C, R1D, R2A, R2B, R2C, R2D, KR,
     N4, N4T, C4, C4T, GP, DF4,
@@ -286,7 +286,7 @@
     OSA, ORA, OSB, ORB, OSC, ORC, OK,
     IRA, ISB, IRB, ISC, IRC, ISD, IRD, IK,
     QSA, QRA, QK, QSB, QG,
-    VEC, UB, VG, SG, RG,
+    VEC, UB, VG, SG, RG, SX, RX,
     ssem, rsem, wss, wrs, gss, grs, hss, hrs,
 ):
     s = lax.axis_index("seq")
@@ -330,6 +330,28 @@
     def wait(ref, sem, flips):
         copy(ref, ref, sem, flips).wait_recv()
 
+    class Tiles:
+        def __init__(self, src, dst, dim, of):
+            self.src, self.dst, self.dim, self.of = src, dst, dim, of
+            self.base = [ids() for _ in of][0] - of[0]
+            self.listed = False
+
+        def each(self, i):
+            return copy(self.src.at[i], self.dst.at[i], self.base + i, (self.dim,))
+
+        def send(self, i):
+            self.each(i).start()
+            if not self.listed:
+                sends.append(self)
+                self.listed = True
+
+        def wait(self, i):
+            self.each(i).wait_recv()
+
+        def wait_send(self):
+            for i in self.of:
+                self.each(i).wait_send()
+
     class Gather:
         def __init__(self, order, block):
             self.order, self.block, self.sem = order, block, {}
@@ -337,10 +359,12 @@
                 for k in itertools.combinations(order, n):
                     self.sem[frozenset(k)] = ids()
 
-        def push(self, *have):
+        def push(self, *have, along=None):
             have = frozenset(have)
             last = max([self.order.index(d) for d in have], default=-1)
             for d in self.order[last + 1 :]:
+                if along and d not in along:
+                    continue
                 ref = self.block(at(have))
                 send(ref, ref, self.sem[have | {d}], (d,))
 
@@ -356,17 +380,27 @@
     barrier = pltpu.get_barrier_semaphore()
 
     def peer(j):
-        b = (me + j) % 32
-        return {"seq": b // 16, "ctx": (b // 2) % 8, "fsdp": b % 2}
-
-    loop(31, lambda j: pl.semaphore_signal(barrier, inc=1, device_id=peer(j + 1), device_id_type=MESH))
+        to = (head + j) % 16
+        return {"seq": to // 8, "ctx": to % 8, "fsdp": x}
+
+    def peer_copy(src, dst, sems, j):
+        return pltpu.make_async_remote_copy(
+            src_ref=src, dst_ref=dst, send_sem=sems[0].at[j], recv_sem=sems[1].at[j],
+            device_id=peer(j % 16), device_id_type=MESH)
+
+    loop(15, lambda j: pl.semaphore_signal(barrier, inc=1, device_id=peer(j + 1), device_id_type=MESH))
+    pl.semaphore_signal(barrier, inc=1, device_id=device("x"), device_id_type=MESH)
 
     X16[s, h, l, y] = tok[...]
+    PK[...] = jnp.zeros_like(PK)
+    for k, vector in enumerate((qb, vb, ob, db, g1, b1, g2, b2)):
+        PK[k // 4, k % 4 * 32 : k % 4 * 32 + 32] = vector[0, :].astype(F32)
+    PK[2, :] = ub[0, :].astype(F32)
     for k in range(HEADS):
         parts = [qkvw[:, j * width + k * HEAD_DIM : j * width + (k + 1) * HEAD_DIM] for j in range(3)]
         WP[k, :, 0 : 3 * HEAD_DIM] = jnp.concatenate(parts, axis=1)
-    WH[me] = WP[head]
-    G[me] = pack[...]
+    WH[head, x] = WP[head]
+    G[head, x] = PK[...]
     OW[h, y, x] = outw[...]
     DW[h, y, x] = downw[...]
 
@@ -376,29 +410,24 @@
     for hp in range(2):
         UW[s, h, l, y, x, :, hp * 512 : (hp + 1) * 512] = upw[:, quarter(s, hp, l)]
 
-    pl.semaphore_wait(barrier, 31)
+    pl.semaphore_wait(barrier, 16)
 
     half = width // 2
 
     def token_block(k):
         return lambda p: X16.at[p["s"], p["h"], p["l"], p["y"], :, pl.ds(k * half, half)]
 
-    xg = [Gather("hyls", token_block(0)), Gather("hlys", token_block(1))]
+    xg = [Gather("hlys", token_block(k)) for k in range(2)]
     for g in xg:
         g.push()
 
     def small_copy(j, dst):
-        b = (me + j) % 32
         return [
-            pltpu.make_async_remote_copy(
-                src_ref=WP.at[b // 2], dst_ref=WH.at[dst], send_sem=wss.at[j], recv_sem=wrs.at[j],
-                device_id=peer(j), device_id_type=MESH),
-            pltpu.make_async_remote_copy(
-                src_ref=pack, dst_ref=G.at[dst], send_sem=gss.at[j], recv_sem=grs.at[j],
-                device_id=peer(j), device_id_type=MESH),
+            peer_copy(WP.at[(head + j) % 16], WH.at[dst, x], (wss, wrs), j),
+            peer_copy(PK, G.at[dst, x], (gss, grs), j),
         ]
 
-    loop(31, lambda j: [d.start() for d in small_copy(j + 1, me)])
+    loop(15, lambda j: [d.start() for d in small_copy(j + 1, head)])
 
     up_sem = {}
     for flips in (("s",), ("l",), ("s", "l")):
@@ -410,55 +439,76 @@
                 UW.at[s, h, l, y, x, :, pl.ds(hp * 512, 512)],
                 up_sem[flips, hp], flips,
             )
+
+    def up_block(k):
+        cols = pl.ds(k * (UW.shape[-1] // 2), UW.shape[-1] // 2)
+        return lambda p: UW.at[:, p["h"], :, p["y"], p["x"], :, cols]
+
+    def down_block(k):
+        rows = pl.ds(k * (DW.shape[-2] // 2), DW.shape[-2] // 2)
+        return lambda p: DW.at[p["h"], p["y"], p["x"], rows]
+
     og = Gather("hyx", lambda p: OW.at[p["h"], p["y"], p["x"]])
-    ug = Gather("hyx", lambda p: UW.at[:, p["h"], :, p["y"], p["x"]])
-    dg = Gather("hyx", lambda p: DW.at[p["h"], p["y"], p["x"]])
+    ug = [Gather("hyx", up_block(0)), Gather("hxy", up_block(1))]
+    dg = [Gather("hyx", down_block(0)), Gather("hxy", down_block(1))]
+    for g in dg:
+        g.push(along="x")
     og.push()
 
-    for g, a, b in ((xg[0], "y", "l"), (xg[1], "l", "y")):
+    for g in xg:
         g.pass_on("h")
     for flips in (("s",), ("l",), ("s", "l")):
         p = at(flips)
         for hp in range(2):
             wait(UW.at[p["s"], h, p["l"], y, x, :, pl.ds(hp * 512, 512)], up_sem[flips, hp], flips)
-    ug.push()
-    xg[0].pass_on("y")
-    xg[1].pass_on("l")
-    xg[0].pass_on("h", "y")
-    xg[1].pass_on("h", "l")
+    for g in ug:
+        g.push()
+    for g in xg:
+        g.pass_on("l")
+
+    def wait_small(j):
+        for d in small_copy(j + 1, (head + 15 - j) % 16):
+            d.wait_recv()
+
+    loop(15, wait_small)
+    small_sem = [ids(), ids()]
+    send(WH.at[:, x], WH.at[:, x], small_sem[0], ("x",))
+    send(G.at[:, x], G.at[:, x], small_sem[1], ("x",))
+    for g in xg:
+        g.pass_on("h", "l")
+    for g in dg:
+        g.push(along="hy")
     og.pass_on("h")
     og.pass_on("y")
     og.pass_on("h", "y")
-    dg.push()
-    for have in (("l",), ("h", "l"), ("y", "l"), ("h", "y", "l")):
-        xg[0].pass_on(*have)
-    for have in (("y",), ("h", "y"), ("l", "y"), ("h", "l", "y")):
-        xg[1].pass_on(*have)
-    ug.pass_on("h")
-    ug.pass_on("y")
-    ug.pass_on("h", "y")
-
-    def wait_small(j):
-        for d in small_copy(j + 1, (me + 31 - j) % 32):
-            d.wait_recv()
-
-    loop(31, wait_small)
+    for have in (("y",), ("l", "y"), ("h", "y"), ("h", "l", "y")):
+        for g in xg:
+            g.pass_on(*have)
+    for g in ug:
+        g.pass_on("h")
+    ug[0].pass_on("y")
+    ug[1].pass_on("x")
+
+    wait(WH.at[:, 1 - x], small_sem[0], ("x",))
+    wait(G.at[:, 1 - x], small_sem[1], ("x",))
 
     spread = [spread_matrix(width, 32, j).astype(BF16) for j in range(4)]
-    mine = own_columns(32, width)
+    block_of, row_at = own_columns(32, width)
+    mine = block_of == row_at
+    arrived = block_of == row_at % 16 * 2 + row_at // 16
     for row, j, to in ((0, 2, 0), (0, 3, 1), (1, 0, 2), (1, 1, 3), (1, 2, 4), (1, 3, 5)):
-        rows = G[:, row, :].astype(BF16)
-        VEC[to : to + 1, :] = jnp.sum(jnp.where(mine, dot(rows, spread[j]), 0.0), axis=0, keepdims=True)
+        rows = jnp.concatenate([G[:, 0, row, :], G[:, 1, row, :]], axis=0).astype(BF16)
+        VEC[to : to + 1, :] = jnp.sum(jnp.where(arrived, dot(rows, spread[j]), 0.0), axis=0, keepdims=True)
     for hp, yp, xp in itertools.product(range(2), repeat=3):
         r = hp * 4 + yp * 2 + xp
-        UB[0:1, r * 128 : (r + 1) * 128] = G[s * 16 + hp * 8 + l * 4 + yp * 2 + xp, 2:3, :]
+        UB[0:1, r * 128 : (r + 1) * 128] = G[s * 8 + hp * 4 + l * 2 + yp, xp, 2:3, :]
     out_bias, down_bias = VEC[0:1, :], VEC[1:2, :]
     gain_one, shift_one, gain_two, shift_two = (VEC[k : k + 1, :] for k in range(2, 6))
-    first, second = G[head * 2, 0:1, :], G[head * 2 + 1, 0:1, :]
+    first, second = G[head, 0, 0:1, :], G[head, 1, 0:1, :]
     head_bias = jnp.concatenate(
         [first[:, 0:32], second[:, 0:32], jnp.zeros((1, 64), F32), first[:, 32:64], second[:, 32:64]], axis=1
     )
-    head_weight = WH[...].reshape(width, WH.shape[2])[:, 0 : 3 * HEAD_DIM]
+    head_weight = WH[...].reshape(width, WH.shape[-1])[:, 0 : 3 * HEAD_DIM]
 
     length = 8 * tok.shape[0]
     qtiles = length // TILE
@@ -494,68 +544,77 @@
 
         loop(qtiles, body)
 
+    tokens = tok.shape[0]
+
+    def tok_cols(hp, lp, yp):
+        return pl.ds(pl.multiple_of((hp * 4 + lp * 2 + yp) * tokens, tokens), tokens)
+
+    others = (("h",), ("y",), ("h", "y"))
+    a_sem = {(f, j): ids() for f in others for j in range(2)}
+
+    def seq_cols(j):
+        sp = s if j == 0 else 1 - s
+        return pl.ds(pl.multiple_of(sp * 2 * tokens, 2 * tokens), 2 * tokens)
+
+    def hand_out(j):
+        for k, flips in enumerate(((),) + others):
+            p = at(flips)
+            piece = jnp.concatenate([OTB[j, :, tok_cols(p["h"], lp, p["y"])] for lp in range(2)], axis=1)
+            if flips:
+                AS[k, j] = piece
+                send(AS.at[k, j], AT.at[h, y, :, seq_cols(j)], a_sem[flips, j], flips)
+            else:
+                AT[h, y, :, seq_cols(j)] = piece
+
     project(0)
     attend(0)
-    for have in (("s",), ("h", "s"), ("y", "s"), ("h", "y", "s"), ("l", "s"), ("h", "l", "s"), ("y", "l", "s"), ("h", "y", "l", "s")):
+    hand_out(0)
+    ug[0].pass_on("h", "y")
+    ug[1].pass_on("h", "x")
+    for have in (("s",), ("h", "s"), ("l", "s"), ("h", "l", "s"), ("y", "s"), ("h", "y", "s"), ("l", "y", "s"), ("h", "l", "y", "s")):
         for g in xg:
             g.pull(*have)
     project(1)
     attend(1)
-    dg.pass_on("h")
-    dg.pass_on("y")
-    dg.pass_on("h", "y")
-
-    tokens = tok.shape[0]
-
-    def tok_cols(hp, lp, yp):
-        return pl.ds(pl.multiple_of((hp * 4 + lp * 2 + yp) * tokens, tokens), tokens)
-
-    others = (("h",), ("y",), ("h", "y"))
-    a_sem = {f: ids() for f in others}
-    for k, flips in enumerate(((),) + others):
-        p = at(flips)
-        for sp, lp in itertools.product(range(2), repeat=2):
-            j = s if sp == 0 else 1 - s
-            to = pl.ds((sp * 2 + lp) * tokens, tokens)
-            piece = OTB[j, :, tok_cols(p["h"], lp, p["y"])]
-            if flips:
-                AS[k, :, to] = piece
-            else:
-                AT[h, y, :, to] = piece
-        if flips:
-            send(AS.at[k], AT.at[h, y], a_sem[flips], flips)
+    hand_out(1)
+    for g in dg:
+        g.pass_on("h")
+    dg[0].pass_on("y")
+    dg[1].pass_on("x")
+    dg[0].pass_on("h", "y")
+    dg[1].pass_on("h", "x")
     for have in (("x",), ("h", "x"), ("y", "x"), ("h", "y", "x")):
         og.pull(*have)
     for flips in others:
         p = at(flips)
-        wait(AT.at[p["h"], p["y"]], a_sem[flips], flips)
+        for j in range(2):
+            wait(AT.at[p["h"], p["y"], :, seq_cols(j)], a_sem[flips, j], flips)
 
     group = 4 * tokens
     A4[...] = AT[...].reshape(4 * HEAD_DIM, group).astype(F32).T.astype(BF16)
 
-    def group_sum(bufs, tile_fn):
+    def group_sum(bufs, tile_fn, meanwhile=None):
         sa, ra, sb, rb = bufs
-        base_a, base_b = [ids() for _ in range(tiles)][0], [ids() for _ in range(tiles)][0]
+        to_core, to_pair = Tiles(sa, ra, "s", range(tiles)), Tiles(sb, rb, "l", range(tiles))
 
         def a(i):
             sa[i] = tile_fn(1 - s, i).astype(BF16)
-            copy(sa.at[i], ra.at[i], base_a + i, ("s",)).start()
+            to_core.send(i)
 
         loop(tiles, a)
 
         def b(i):
             v = tile_fn(s, i)
-            wait(ra.at[i], base_a + i, ("s",))
+            to_core.wait(i)
             KR[i] = (v + ra[i].astype(F32)).reshape(2, tokens, TILE)
             sb[i] = KR[i, 1 - l].astype(BF16)
-            copy(sb.at[i], rb.at[i], base_b + i, ("l",)).start()
+            to_pair.send(i)
 
         loop(tiles, b)
+        if meanwhile is not None:
+            meanwhile()
         for i in range(tiles):
-            wait(rb.at[i], base_b + i, ("l",))
-        for i in range(tiles):
-            sends.append(copy(sa.at[i], ra.at[i], base_a + i, ("s",)))
-            sends.append(copy(sb.at[i], rb.at[i], base_b + i, ("l",)))
+            to_pair.wait(i)
         return jnp.concatenate([KR[i, l] + rb[i].astype(F32) for i in range(tiles)], axis=1)
 
     def group_rows(sp):
@@ -606,8 +665,13 @@
     group_gather(N4, first_norm.astype(BF16))
     settle(mark)
 
-    for have in (("x",), ("h", "x"), ("y", "x"), ("h", "y", "x")):
-        ug.pull(*have)
+    def pull_rest(pair):
+        for have in (("x",), ("h", "x"), ("y", "x"), ("h", "y", "x")):
+            pair[0].pull(*have)
+        for have in (("y",), ("h", "y"), ("x", "y"), ("h", "x", "y")):
+            pair[1].pull(*have)
+
+    pull_rest(ug)
     hidden = UB.shape[1]
 
     def all_rows(ref):
@@ -623,8 +687,7 @@
         C4[:, cols] = act.astype(BF16)
 
     loop(hidden // TILE, up)
-    for have in (("x",), ("h", "x"), ("y", "x"), ("h", "y", "x")):
-        dg.pull(*have)
+    pull_rest(dg)
     feed = group_sum(
         (R2A, R2B, R2C, R2D),
         lambda sp, i: dot(C4[group_rows(sp), :], DW[:, :, :, :, col_tile(i)].reshape(hidden, TILE)),
@@ -658,13 +721,83 @@
         DH4[:, cols] = v
         UB[1:2, cols] = jnp.sum(v.astype(F32), axis=0, keepdims=True)
 
+    class Scatter:
+        def __init__(self, bufs, product):
+            self.sa, self.ra, self.sb, self.rb, self.sc, self.rc, self.keep = bufs
+            self.product = product
+            self.shape = self.sa.shape[1:]
+            self.parts = []
+            for k, (one, two) in enumerate((("x", "y"), ("y", "x"))):
+                of = range(k * tiles // 2, (k + 1) * tiles // 2)
+                self.parts.append((
+                    one, two, of,
+                    Tiles(self.sa, self.ra, one, of), Tiles(self.sb, self.rb, two, of), Tiles(self.sc, self.rc, "h", of),
+                ))
+
+        def first(self):
+            for one, two, of, a, b, c in self.parts:
+                def body(i, one=one, of=of, a=a):
+                    i = of[0] + i
+                    self.sa[i] = self.product(one, 1 - here[one], i).reshape(self.shape).astype(BF16)
+                    a.send(i)
+
+                loop(len(of), body)
+
+        def second(self):
+            for one, two, of, a, b, c in self.parts:
+                def body(i, one=one, two=two, of=of, a=a, b=b):
+                    i = of[0] + i
+                    v = self.product(one, here[one], i).reshape(self.shape)
+                    a.wait(i)
+                    self.keep[i] = v + self.ra[i].astype(F32)
+                    self.sb[i] = self.keep[i, :, 1 - here[two]].astype(BF16)
+                    b.send(i)
+
+                loop(len(of), body)
+
+        def third(self):
+            for one, two, of, a, b, c in self.parts:
+                def body(i, two=two, of=of, b=b, c=c):
+                    i = of[0] + i
+                    b.wait(i)
+                    self.keep[i, :, 0] = self.keep[i, :, here[two]] + self.rb[i].astype(F32)
+                    self.sc[i] = self.keep[i, 1 - h, 0].astype(BF16)
+                    c.send(i)
+
+                loop(len(of), body)
+
+        def last(self, out):
+            for one, two, of, a, b, c in self.parts:
+                def body(i, of=of, c=c):
+                    i = of[0] + i
+                    c.wait(i)
+                    out[:, col_tile(i)] = self.keep[i, h, 0] + self.rc[i].astype(F32)
+
+                loop(len(of), body)
+
+    def up_product(dim, v, i):
+        rows = N4T[:, :, v] if dim == "x" else N4T[:, v]
+        return dot(rows.reshape(group, group), DH4[:, col_tile(i)])
+
+    def down_product(dim, v, i):
+        rows = C4T[:, :, v] if dim == "x" else C4T[:, v]
+        return dot(rows.reshape(group, group), DF4[:, :, :, col_tile(i)].reshape(group, TILE))
+
+    def out_product(dim, v, i):
+        rows = AT[:, :, pl.ds(pl.multiple_of(v * 32, 32), 32), :] if dim == "x" else AT[:, v]
+        return dot(rows.reshape(128, group), DB4[:, :, :, col_tile(i)].reshape(group, TILE))
+
+    down_s = Scatter((DSA, DRA, DSB, DRB, DSC, DRC, DK), down_product)
+    up_s = Scatter((USA, URA, USB, URB, USC, URC, UK), up_product)
+    out_s = Scatter((OSA, ORA, OSB, ORB, OSC, ORC, OK), out_product)
+
     loop(hidden // TILE, d_hidden)
 
     def up_rows(i):
         return UW[i // 2, i % 2].reshape(TILE, hidden)
 
     d_first = group_sum(
-        (R1A, R1B, R1C, R1D), lambda sp, i: dot(DH4[group_rows(sp), :], up_rows(i), 1, 1)
+        (R1A, R1B, R1C, R1D), lambda sp, i: dot(DH4[group_rows(sp), :], up_rows(i), 1, 1), down_s.first
     )
     d_sum_one, gain_one_grad, shift_one_grad = norm_backward(
         DSEC[...] + d_first, NORM1[...], recip_one, gain_one
@@ -674,7 +807,7 @@
     VG[0:1, :] = jnp.sum(d_branch.astype(F32), axis=0, keepdims=True)
     VG[2:3, :] = gain_one_grad
     VG[3:4, :] = shift_one_grad
-    group_gather(DB4, d_branch)
+    group_gather(DB4, d_branch, up_s.first)
 
     d_att = dot(all_rows(DB4), OW[...].reshape(4 * HEAD_DIM, width), 1, 1).astype(BF16)
     d_att = d_att.astype(F32).T.astype(BF16).reshape(2, 2, HEAD_DIM, group)
@@ -685,75 +818,8 @@
         send(DS.at[p["h"], p["y"]], DR.at[h, y], d_sem[flips], flips)
     DR[h, y] = DS[h, y]
 
-    class Scatter:
-        def __init__(self, bufs, product):
-            self.sa, self.ra, self.sb, self.rb, self.sc, self.rc, self.keep = bufs
-            self.product = product
-            self.a, self.b, self.c = ([ids() for _ in range(tiles)][0] for _ in range(3))
-            self.shape = self.sa.shape[1:]
-
-        def done(self, src, dst, base, dim):
-            for i in range(tiles):
-                sends.append(copy(src.at[i], dst.at[i], base + i, (dim,)))
-
-        def first(self):
-            def body(i):
-                self.sa[i] = self.product(1 - x, i).reshape(self.shape).astype(BF16)
-                copy(self.sa.at[i], self.ra.at[i], self.a + i, ("x",)).start()
-
-            loop(tiles, body)
-            self.done(self.sa, self.ra, self.a, "x")
-
-        def second(self):
-            def body(i):
-                v = self.product(x, i).reshape(self.shape)
-                wait(self.ra.at[i], self.a + i, ("x",))
-                self.keep[i] = v + self.ra[i].astype(F32)
-                self.sb[i] = self.keep[i, :, 1 - y].astype(BF16)
-                copy(self.sb.at[i], self.rb.at[i], self.b + i, ("y",)).start()
-
-            loop(tiles, body)
-            self.done(self.sb, self.rb, self.b, "y")
-
-        def third(self):
-            def body(i):
-                wait(self.rb.at[i], self.b + i, ("y",))
-                self.keep[i, :, 0] = self.keep[i, :, y] + self.rb[i].astype(F32)
-                self.sc[i] = self.keep[i, 1 - h, 0].astype(BF16)
-                copy(self.sc.at[i], self.rc.at[i], self.c + i, ("h",)).start()
-
-            loop(tiles, body)
-            self.done(self.sc, self.rc, self.c, "h")
-
-        def last(self, out):
-            def body(i):
-                wait(self.rc.at[i], self.c + i, ("h",))
-                out[:, col_tile(i)] = self.keep[i, h, 0] + self.rc[i].astype(F32)
-
-            loop(tiles, body)
-
-    def up_product(xp, i):
-        return dot(N4T[:, :, xp].reshape(group, group), DH4[:, col_tile(i)])
-
-    def down_product(xp, i):
-        return dot(
-            C4T[:, :, xp].reshape(group, group),
-            DF4[:, :, :, col_tile(i)].reshape(group, TILE),
-        )
-
-    def out_product(xp, i):
-        rows = pl.ds(pl.multiple_of(xp * 32, 32), 32)
-        return dot(
-            AT[:, :, rows, :].reshape(128, group),
-            DB4[:, :, :, col_tile(i)].reshape(group, TILE),
-        )
-
-    down_s = Scatter((DSA, DRA, DSB, DRB, DSC, DRC, DK), down_product)
-    up_s = Scatter((USA, URA, USB, URB, USC, URC, UK), up_product)
-    out_s = Scatter((OSA, ORA, OSB, ORB, OSC, ORC, OK), out_product)
-    down_s.first()
-    up_s.first()
     out_s.first()
+    down_s.second()
 
     for flips in others:
         p = at(flips)
@@ -791,28 +857,24 @@
         DQKVT[j, 128:192, :] = dv.T.astype(BF16)
         return jnp.sum(dq, axis=0, keepdims=True), jnp.sum(dv, axis=0, keepdims=True)
 
-    q0, v0 = attend_back(0)
-    down_s.second()
+    def input_tile(j, i):
+        w = WH[pl.ds(pl.multiple_of(i * 4, 4), 4)].reshape(TILE, WH.shape[-1])[:, 0 : 3 * HEAD_DIM]
+        return dot(DQKV[j], w, 1, 1).reshape(2, 2, 2, tokens, TILE)
+
+    ia, ib, ic, id_ = ([ids() for _ in range(tiles)][0] for _ in range(4))
+
+    def in_sent(i):
+        return (C4T if i < tiles // 2 else N4T).at[:, :, :, :, pl.ds(i % 2 * TILE, TILE)]
+
     q1, v1 = attend_back(1)
     up_s.second()
-    out_s.second()
-    down_s.third()
-    up_s.third()
-
-    def input_tile(j, i):
-        w = WH[pl.ds(pl.multiple_of(i * 8, 8), 8)].reshape(TILE, WH.shape[2])[:, 0 : 3 * HEAD_DIM]
-        return dot(DQKV[j], w, 1, 1).reshape(2, 2, 2, tokens, TILE)
-
-    ia, ib, ic, id_ = ([ids() for _ in range(tiles)][0] for _ in range(4))
-
-    def in_sent(i):
-        return (C4T if i < tiles // 2 else N4T).at[:, :, :, :, pl.ds(i % 2 * TILE, TILE)]
-
     for i in range(tiles):
         in_sent(i)[...] = input_tile(1, i).astype(BF16)
         send(in_sent(i), IRA.at[i], ia + i, ("s",))
-
-    qa = [ids() for _ in range(tiles)][0]
+    q0, v0 = attend_back(0)
+    out_s.second()
+
+    to_x = Tiles(QSA, QRA, "x", range(tiles))
 
     def q_first(i):
         cols = col_tile(i)
@@ -822,7 +884,7 @@
         for xp in range(2):
             QK[i, xp] = v[:, :, xp]
         QSA[i, :, :, :, 0 : 3 * HEAD_DIM] = QK[i, 1 - x].astype(BF16)
-        copy(QSA.at[i], QRA.at[i], qa + i, ("x",)).start()
+        to_x.send(i)
 
     for i in range(tiles):
         dims = ("l", "y") if i < tiles // 2 else ("y", "l")
@@ -831,7 +893,7 @@
         ISB[i] = (IK[i, :, 1 - l] if dims[0] == "l" else IK[i, :, :, 1 - y]).astype(BF16)
         send(ISB.at[i], IRB.at[i], ib + i, (dims[0],))
     loop(tiles, q_first)
-    out_s.third()
+    down_s.third()
 
     bq, bv = q0 + q1, v0 + v1
     VG[6:8, :] = jnp.zeros((2, width), F32)
@@ -855,16 +917,13 @@
         SG[b, 0:1, :] += jnp.concatenate([bq[:, lanes], bv[:, lanes], jnp.zeros((1, 64), F32)], axis=1)
     for hp, yp, xp in itertools.product(range(2), repeat=3):
         r = hp * 4 + yp * 2 + xp
-        SG[s * 16 + hp * 8 + l * 4 + yp * 2 + xp, 2:3, :] = UB[1:2, r * 128 : (r + 1) * 128]
+        SG[(s * 8 + hp * 4 + l * 2 + yp) * 2 + xp, 2:3, :] = UB[1:2, r * 128 : (r + 1) * 128]
 
     def grad_copy(j):
-        b = (me + j) % 32
-        return pltpu.make_async_remote_copy(
-            src_ref=SG.at[b], dst_ref=RG.at[j], send_sem=hss.at[j], recv_sem=hrs.at[j],
-            device_id=peer(j), device_id_type=MESH)
-
-    loop(31, lambda j: grad_copy(j + 1).start())
-    RG[0] = SG[me]
+        return peer_copy(SG.at[pl.ds((head + j) % 16 * 2, 2)], RG.at[j], (hss, hrs), j)
+
+    loop(15, lambda j: grad_copy(j + 1).start())
+    RG[0] = SG[pl.ds(head * 2, 2)]
 
     for i in range(tiles):
         dims = ("l", "y") if i < tiles // 2 else ("y", "l")
@@ -880,25 +939,29 @@
         send(ISC.at[i], IRC.at[i], ic + i, (dims[1],))
 
     def q_second(i):
-        wait(QRA.at[i], qa + i, ("x",))
+        to_x.wait(i)
         v = QK[i, x] + QRA[i, :, :, :, 0 : 3 * HEAD_DIM].astype(F32)
         QSB[i // 2, i % 2, :, :, :, 0 : 3 * HEAD_DIM] = v.astype(BF16)
 
     loop(tiles, q_second)
-    for i in range(tiles):
-        sends.append(copy(QSA.at[i], QRA.at[i], qa + i, ("x",)))
 
     def piece_copy(j):
         to = (head + j) % 16
-        return pltpu.make_async_remote_copy(
-            src_ref=QSB.at[to // 8, (to // 4) % 2, (to // 2) % 2, to % 2], dst_ref=QG.at[head],
-            send_sem=hss.at[32 + j], recv_sem=hrs.at[32 + j],
-            device_id={"seq": to // 8, "ctx": to % 8, "fsdp": x}, device_id_type=MESH)
+        return peer_copy(
+            QSB.at[to // 8, (to // 4) % 2, (to // 2) % 2, to % 2], QG.at[head], (hss, hrs), 16 + j
+        )
 
     loop(15, lambda j: piece_copy(j + 1).start())
     QG[head] = QSB[s, h, l, y]
 
+    up_s.third()
+    out_s.third()
     down_s.last(downg_o)
+    loop(15, lambda j: grad_copy(j + 1).wait_recv())
+    small_sum = jnp.sum(RG[...], axis=0)
+    SX[0:2] = small_sum
+    x_sem = ids()
+    send(SX.at[1 - x], RX, x_sem, ("x",))
     up_s.last(UF)
     uf_sem = {}
     for flips in (("s",), ("l",), ("s", "l")):
@@ -921,8 +984,8 @@
         send(ISD.at[i], IRD.at[i], id_ + i, ("h",))
     out_s.last(outg_o)
 
-    loop(31, lambda j: grad_copy(j + 1).wait_recv())
-    small_o[...] = jnp.sum(RG[...], axis=0)
+    wait(RX, x_sem, ("x",))
+    small_o[...] = SX[x] + RX[...]
 
     loop(15, lambda j: piece_copy(j + 1).wait_recv())
     for k in range(HEADS // 2):
@@ -946,12 +1009,24 @@
         d.wait_send()
 
     def small_sent(j):
-        for d in small_copy(j + 1, me):
+        for d in small_copy(j + 1, head):
             d.wait_send()
         grad_copy(j + 1).wait_send()
 
-    loop(31, small_sent)
+    loop(15, small_sent)
     loop(15, lambda j: piece_copy(j + 1).wait_send())
+
+
+def hand_over(*refs):
+    large, small, outs, sems = refs[:6], refs[6], refs[7:22], refs[22]
+    copies = [pltpu.make_async_copy(a, b, sems.at[k]) for k, (a, b) in enumerate(zip(large, outs))]
+    for c in copies:
+        c.start()
+    places = ((0, 0, 32), (0, 32, 32), (0, 64, 32), (2, 0, 128), (0, 96, 32), (1, 0, 32), (1, 32, 32), (1, 64, 32), (1, 96, 32))
+    for ref, (row, lane, count) in zip(outs[6:], places):
+        ref[...] = small[row : row + 1, lane : lane + count]
+    for c in copies:
+        c.wait()
 
 
 def on_block(
@@ -964,10 +1039,10 @@
     group = 4 * n
     length = 8 * n
     tiles = width // TILE
-    small = jnp.concatenate(
-        [query_bias, value_bias, out_bias, down_bias, norm1_gain, norm1_bias, norm2_gain, norm2_bias, up_bias]
-    ).astype(F32).reshape(3, 128)
-    pack = jnp.pad(small, ((0, 5), (0, 0)))
+    vectors = [
+        v.reshape(1, -1)
+        for v in (query_bias, value_bias, out_bias, up_bias, down_bias, norm1_gain, norm1_bias, norm2_gain, norm2_bias)
+    ]
 
     def b(*shape):
         return pltpu.VMEM(shape, BF16)
@@ -987,10 +1062,10 @@
 
     sem = pltpu.SemaphoreType.DMA
     scratch = [
-        b(2, 2, 2, 2, n, width), b(HEADS, 32, 256), b(32, 32, 256), f(32, 8, 128),
+        f(8, 128), b(2, 2, 2, 2, n, width), b(HEADS, 32, 256), b(HEADS, 2, 32, 256), f(HEADS, 2, 8, 128),
         b(2, 2, 2, 32, width), b(2, 2, 2, 2, 2, 32, hidden), b(2, 2, 2, 128, width),
         b(2, length, 64), b(2, length, 64), b(2, length, 64), b(2, 192, length), f(2, 64, length), b(2, 64, length),
-        f(2, 8, length), b(4, 64, group), b(2, 2, 64, group), b(group, 256),
+        f(2, 8, length), b(4, 2, 64, group // 2), b(2, 2, 64, group), b(group, 256),
         *group_bufs, *group_bufs, f(tiles, 2, n, TILE),
         b(2, 2, n, width), b(2, 2, 2, 128, group), b(group, hidden), b(2, 2, 2, 128, group), f(group, hidden),
         b(2, 2, n, width),
@@ -1003,8 +1078,8 @@
         b(tiles, 2, 2, 2, n, TILE), b(tiles, 2, 2, n, TILE), b(tiles, 2, 2, n, TILE),
         b(tiles, 2, n, TILE), b(tiles, 2, n, TILE), b(tiles, n, TILE), b(tiles, n, TILE), f(tiles, 2, 2, 2, n, TILE),
         b(tiles, 2, 2, 32, 256), b(tiles, 2, 2, 32, 256), f(tiles, 2, 2, 2, 32, 192), b(2, 2, 2, 2, 32, 256), b(HEADS, 32, 256),
-        f(8, width), f(8, hidden), f(8, width), f(32, 8, 128), f(32, 8, 128),
-        sem((256,)), sem((256,)), sem((32,)), sem((32,)), sem((32,)), sem((32,)), sem((48,)), sem((48,)),
+        f(8, width), f(8, hidden), f(8, width), f(32, 8, 128), f(HEADS, 2, 8, 128), f(2, 8, 128), f(8, 128),
+        sem((300,)), sem((300,)), sem((16,)), sem((16,)), sem((16,)), sem((16,)), sem((32,)), sem((32,)),
     ]
     vmem = pl.BlockSpec(memory_space=pltpu.VMEM)
     shapes = [
@@ -1016,22 +1091,29 @@
         jax.ShapeDtypeStruct((128, width), F32),
         jax.ShapeDtypeStruct((8, 128), F32),
     ]
-    out, ig, qkvg, outg, upg, downg, sm = pl.pallas_call(
+    results = pl.pallas_call(
         layer_kernel,
         out_shape=shapes,
-        in_specs=[vmem] * 7,
+        in_specs=[vmem] * 15,
         out_specs=[vmem] * 7,
         scratch_shapes=scratch,
         compiler_params=pltpu.CompilerParams(
             collective_id=0, has_side_effects=True, vmem_limit_bytes=63 * 2**20
         ),
         name="layer",
-    )(tokens[0], qkv_weight, out_weight, up_weight, down_weight, pack, cotangent[0])
-    row0, row1 = sm[0], sm[1]
+    )(tokens[0], qkv_weight, out_weight, up_weight, down_weight, *vectors, cotangent[0])
+    lengths = [v.shape[1] for v in vectors]
+    everywhere = pl.BlockSpec(memory_space=pl.ANY)
+    done = pl.pallas_call(
+        hand_over,
+        out_shape=shapes[:6] + [jax.ShapeDtypeStruct((1, k), F32) for k in lengths],
+        in_specs=[vmem] * 7,
+        out_specs=[everywhere] * 6 + [vmem] * 9,
+        scratch_shapes=[sem((6,))],
+        name="results",
+    )(*results)
     return (
-        out[None], ig[None], qkvg, outg, upg, downg,
-        row0[0:32], row0[32:64], row0[64:96], sm[2], row0[96:128],
-        row1[0:32], row1[32:64], row1[64:96], row1[96:128],
+        done[0][None], done[1][None], *done[2:6], *(v.reshape(-1) for v in done[6:]),
     )
 
 

time: 270 us -> 226 us (0.84)
  Pallas kernels: 254 us -> 223 us
  local copies, waits for them, and re-layouts: 14 us -> 0 us
    pallas_call x1 -> x2, Pallas kernels: 254 us -> 223 us  [the longest x1 219 us: on_block(): pl.pallas_call(layer_kernel, out_shape=shapes, in_specs=[vmem] * 15, out_...]
    unnamed x22 -> x0, local copies, waits for them, and re-layouts: 7.2 us -> none
    concatenate x1 -> x0, local copies, waits for them, and re-layouts: 4.09 us -> none  [on_block(): jnp.concatenate([query_bias, value_bias, out_bias, down_bias, norm1_gain,...]
where the time goes in v2:
time: 226 us; the launch traced here: 224 us
  Pallas kernels  223 us (99%)
    pallas_call x1, Pallas kernels, on_block(): pl.pallas_call(layer_kernel, out_shape=shapes, in_specs=[vmem] * 15, out_...  219 us

profile of v2, /device:TPU:1, one launch (start us, length us, event | category | flops | bytes accessed | tf_op | source)
XLA Modules:
  0.0 223.8 jit_solution(6645678572584837772)
XLA Ops:
  0.7 219.3 %layer.1 = (bf16[128,1024]{1,0:T(8,128)(2,1)}, f32[128,1024]{1,0:T(8,128)}, f32[32,3072]{1,0:T(8,128)}, f32[32,1024]{1,0:T(8,128)}, f32[32,4096]{1,0:T(8,128)}, /*index=5*/f32[128,1024]{1,0:T(8,128)}, f32[8,128]{1,0:T(8,128)}) custom-call(bf16[128,1024]{1,0:T(8,128)(2,1)} %bitcast.22, bf16[32,3072]{1,0:T(8,128)(2,1)} %qkvw.1, bf16[32,1024]{1,0:T(8,128)(2,1)} %outw.1, ...), custom_call_target="tpu_custom_call" | custom-call | tf_op jit(solution)/shard_map/layer/pallas_call | solution.py:1094
  220.0 3.6 %results.1 = (bf16[128,1024]{1,0:T(8,128)(2,1)}, f32[128,1024]{1,0:T(8,128)}, f32[32,3072]{1,0:T(8,128)}, f32[32,1024]{1,0:T(8,128)}, f32[32,4096]{1,0:T(8,128)}...) custom-call(bf16[128,1024]{1,0:T(8,128)(2,1)} %get-tuple-element.37., ...), custom_call_target="tpu_custom_call" | custom-call | tf_op jit(solution)/shard_map/results/pallas_call | solution.py:1107

commit v3 on v2

--- a/solution.py
+++ b/solution.py
@@ -417,7 +417,7 @@
     def token_block(k):
         return lambda p: X16.at[p["s"], p["h"], p["l"], p["y"], :, pl.ds(k * half, half)]
 
-    xg = [Gather("hlys", token_block(k)) for k in range(2)]
+    xg = [Gather("hlys", token_block(0)), Gather("hyls", token_block(1))]
     for g in xg:
         g.push()
 
@@ -441,11 +441,11 @@
             )
 
     def up_block(k):
-        cols = pl.ds(k * (UW.shape[-1] // 2), UW.shape[-1] // 2)
+        cols = (pl.ds(0, UW.shape[-1] // 2), pl.ds(UW.shape[-1] // 2, UW.shape[-1] // 2))[k]
         return lambda p: UW.at[:, p["h"], :, p["y"], p["x"], :, cols]
 
     def down_block(k):
-        rows = pl.ds(k * (DW.shape[-2] // 2), DW.shape[-2] // 2)
+        rows = (pl.ds(0, DW.shape[-2] // 2), pl.ds(DW.shape[-2] // 2, DW.shape[-2] // 2))[k]
         return lambda p: DW.at[p["h"], p["y"], p["x"], rows]
 
     og = Gather("hyx", lambda p: OW.at[p["h"], p["y"], p["x"]])
@@ -463,8 +463,8 @@
             wait(UW.at[p["s"], h, p["l"], y, x, :, pl.ds(hp * 512, 512)], up_sem[flips, hp], flips)
     for g in ug:
         g.push()
-    for g in xg:
-        g.pass_on("l")
+    xg[0].pass_on("l")
+    xg[1].pass_on("y")
 
     def wait_small(j):
         for d in small_copy(j + 1, (head + 15 - j) % 16):
@@ -474,15 +474,16 @@
     small_sem = [ids(), ids()]
     send(WH.at[:, x], WH.at[:, x], small_sem[0], ("x",))
     send(G.at[:, x], G.at[:, x], small_sem[1], ("x",))
-    for g in xg:
-        g.pass_on("h", "l")
+    xg[0].pass_on("h", "l")
+    xg[1].pass_on("h", "y")
     for g in dg:
         g.push(along="hy")
     og.pass_on("h")
     og.pass_on("y")
     og.pass_on("h", "y")
-    for have in (("y",), ("l", "y"), ("h", "y"), ("h", "l", "y")):
-        for g in xg:
+    for a, b in (("y", "l"), ("l", "y")):
+        g = xg[0] if a == "y" else xg[1]
+        for have in ((a,), ("h", a), (b, a), ("h", b, a)):
             g.pass_on(*have)
     for g in ug:
         g.pass_on("h")
@@ -591,43 +592,69 @@
             wait(AT.at[p["h"], p["y"], :, seq_cols(j)], a_sem[flips, j], flips)
 
     group = 4 * tokens
-    A4[...] = AT[...].reshape(4 * HEAD_DIM, group).astype(F32).T.astype(BF16)
-
-    def group_sum(bufs, tile_fn, meanwhile=None):
-        sa, ra, sb, rb = bufs
-        to_core, to_pair = Tiles(sa, ra, "s", range(tiles)), Tiles(sb, rb, "l", range(tiles))
-
-        def a(i):
-            sa[i] = tile_fn(1 - s, i).astype(BF16)
-            to_core.send(i)
-
-        loop(tiles, a)
-
-        def b(i):
-            v = tile_fn(s, i)
-            to_core.wait(i)
-            KR[i] = (v + ra[i].astype(F32)).reshape(2, tokens, TILE)
-            sb[i] = KR[i, 1 - l].astype(BF16)
-            to_pair.send(i)
-
-        loop(tiles, b)
-        if meanwhile is not None:
-            meanwhile()
-        for i in range(tiles):
-            to_pair.wait(i)
-        return jnp.concatenate([KR[i, l] + rb[i].astype(F32) for i in range(tiles)], axis=1)
-
-    def group_rows(sp):
-        return pl.ds(pl.multiple_of(sp * 2 * tokens, 2 * tokens), 2 * tokens)
+    half_n = tokens // 2
+    A4[...] = AT[...].reshape(4 * HEAD_DIM, group).astype(F32).T.astype(BF16).reshape(A4.shape)
+
+    def rows_of(k):
+        return slice(k * half_n, (k + 1) * half_n)
+
+    def half_rows(ref, k):
+        return ref[:, :, rows_of(k), :].reshape(4 * half_n, ref.shape[-1])
+
+    def core_rows(ref, k, sp):
+        return ref[sp, :, rows_of(k), :].reshape(2 * half_n, ref.shape[-1])
+
+    class GroupSum:
+        def __init__(self, bufs, ref, product):
+            self.sa, self.ra, self.sb, self.rb = bufs
+            self.ref, self.product = ref, product
+            self.to_core = [Tiles(self.sa.at[k], self.ra.at[k], "s", range(tiles)) for k in range(2)]
+            self.to_pair = [Tiles(self.sb.at[k], self.rb.at[k], "l", range(tiles)) for k in range(2)]
+
+        def start(self, k):
+            def body(i):
+                left = jnp.concatenate([core_rows(self.ref, k, 1 - s), core_rows(self.ref, k, s)], axis=0)
+                v = self.product(left, i).reshape(2, 2, half_n, TILE)
+                self.sa[k, i] = v[0].astype(BF16)
+                self.to_core[k].send(i)
+                KR[k, i] = v[1]
+
+            loop(tiles, body)
+
+        def relay(self, k):
+            def body(i):
+                self.to_core[k].wait(i)
+                KR[k, i] += self.ra[k, i].astype(F32)
+                self.sb[k, i] = KR[k, i, 1 - l].astype(BF16)
+                self.to_pair[k].send(i)
+
+            loop(tiles, body)
+
+        def finish(self, k):
+            for i in range(tiles):
+                self.to_pair[k].wait(i)
+            return jnp.concatenate([KR[k, i, l] + self.rb[k, i].astype(F32) for i in range(tiles)], axis=1)
+
+    class GroupGather:
+        def __init__(self, ref):
+            self.ref = ref
+            self.half = [
+                Gather("ls", lambda p, k=k: ref.at[p["s"], p["l"], pl.ds(k * half_n, half_n)]) for k in range(2)
+            ]
+
+        def push(self, k, value):
+            self.ref[s, l, rows_of(k)] = value
+            self.half[k].push()
+
+        def relay(self, k):
+            self.half[k].pass_on("l")
+
+        def pull(self, k):
+            self.half[k].pull("s")
+            self.half[k].pull("l", "s")
 
     def col_tile(i):
         return pl.ds(pl.multiple_of(i * TILE, TILE), TILE)
-
-    mark = len(sends)
-    branch = group_sum(
-        (R1A, R1B, R1C, R1D),
-        lambda sp, i: dot(A4[group_rows(sp), :], OW[:, :, :, :, col_tile(i)].reshape(4 * HEAD_DIM, TILE)),
-    )
 
     def norm_forward(values, gain, shift):
         centered = values - jnp.mean(values, axis=-1, keepdims=True)
@@ -646,24 +673,31 @@
         )
         return recip * inner, gain_grad, shift_grad
 
-    first_norm, normal_one, recip_one = norm_forward(
-        tok[...].astype(F32) + branch + out_bias, gain_one, shift_one
-    )
-    FN[...] = first_norm
-    NORM1[...] = normal_one
-
-    def group_gather(ref, value, meanwhile=None):
-        g = Gather("ls", lambda p: ref.at[p["s"], p["l"]])
-        ref[s, l] = value
-        g.push()
-        if meanwhile is not None:
-            meanwhile()
-        g.pass_on("l")
-        g.pull("s")
-        g.pull("l", "s")
-
-    group_gather(N4, first_norm.astype(BF16))
-    settle(mark)
+    def add_vectors(k, first_row, *rows):
+        for at_row, row in zip(first_row, rows):
+            VG[at_row : at_row + 1, :] = row if k == 0 else VG[at_row : at_row + 1, :] + row
+
+    mark = len(sends)
+    branch = GroupSum(
+        (R1A, R1B, R1C, R1D), A4,
+        lambda left, i: dot(left, OW[:, :, :, :, col_tile(i)].reshape(4 * HEAD_DIM, TILE)),
+    )
+    branch.start(0)
+    branch.start(1)
+    branch.relay(0)
+    branch.relay(1)
+
+    normed = GroupGather(N4)
+    recips = []
+    for k in range(2):
+        r = rows_of(k)
+        first_norm, normal_one, recip_one = norm_forward(
+            tok[r, :].astype(F32) + branch.finish(k) + out_bias, gain_one, shift_one
+        )
+        FN[r, :] = first_norm
+        NORM1[r, :] = normal_one
+        recips.append(recip_one)
+        normed.push(k, first_norm.astype(BF16))
 
     def pull_rest(pair):
         for have in (("x",), ("h", "x"), ("y", "x"), ("h", "y", "x")):
@@ -671,37 +705,54 @@
         for have in (("y",), ("h", "y"), ("x", "y"), ("h", "x", "y")):
             pair[1].pull(*have)
 
+    hidden = UB.shape[1]
+
+    def up(k):
+        def body(i):
+            cols = col_tile(i)
+            w = UW[:, :, :, :, :, :, cols].reshape(width, TILE)
+            pre = dot(half_rows(N4, k), w) + UB[0:1, cols]
+            phi = 0.5 * (1.0 + lax.erf(pre * (2.0 ** -0.5)))
+            slope = phi + pre * (jnp.exp(-0.5 * pre * pre) * ((2.0 * math.pi) ** -0.5))
+            GP[:, :, rows_of(k), cols] = slope.reshape(2, 2, half_n, TILE)
+            C4[:, :, rows_of(k), cols] = (pre * phi).astype(BF16).reshape(2, 2, half_n, TILE)
+
+        loop(hidden // TILE, body)
+
+    feed = GroupSum(
+        (R2A, R2B, R2C, R2D), C4,
+        lambda left, i: dot(left, DW[:, :, :, :, col_tile(i)].reshape(hidden, TILE)),
+    )
+    normed.relay(0)
     pull_rest(ug)
-    hidden = UB.shape[1]
-
-    def all_rows(ref):
-        return ref[...].reshape(group, ref.shape[-1])
-
-    def up(i):
-        cols = col_tile(i)
-        w = UW[:, :, :, :, :, :, cols].reshape(width, TILE)
-        pre = dot(all_rows(N4), w) + UB[0:1, cols]
-        phi = 0.5 * (1.0 + lax.erf(pre * (2.0 ** -0.5)))
-        act = pre * phi
-        GP[:, cols] = phi + pre * (jnp.exp(-0.5 * pre * pre) * ((2.0 * math.pi) ** -0.5))
-        C4[:, cols] = act.astype(BF16)
-
-    loop(hidden // TILE, up)
+    normed.pull(0)
+    up(0)
+    normed.relay(1)
     pull_rest(dg)
-    feed = group_sum(
-        (R2A, R2B, R2C, R2D),
-        lambda sp, i: dot(C4[group_rows(sp), :], DW[:, :, :, :, col_tile(i)].reshape(hidden, TILE)),
-    )
-    final, normal_two, recip_two = norm_forward(FN[...] + feed + down_bias, gain_two, shift_two)
-    out_o[...] = final.astype(BF16)
-    d_second, gain_two_grad, shift_two_grad = norm_backward(
-        cot[...].astype(F32), normal_two, recip_two, gain_two
-    )
-    DSEC[...] = d_second
-    d_feed = d_second.astype(BF16)
-    VG[1:2, :] = jnp.sum(d_feed.astype(F32), axis=0, keepdims=True)
-    VG[4:5, :] = gain_two_grad
-    VG[5:6, :] = shift_two_grad
+    feed.start(0)
+    normed.pull(1)
+    up(1)
+    feed.relay(0)
+    feed.start(1)
+    feed.relay(1)
+    settle(mark)
+
+    d_feeds = GroupGather(DF4)
+    for k in range(2):
+        r = rows_of(k)
+        final, normal_two, recip_two = norm_forward(
+            FN[r, :] + feed.finish(k) + down_bias, gain_two, shift_two
+        )
+        out_o[r, :] = final.astype(BF16)
+        d_second, gain_two_grad, shift_two_grad = norm_backward(
+            cot[r, :].astype(F32), normal_two, recip_two, gain_two
+        )
+        DSEC[r, :] = d_second
+        d_feed = d_second.astype(BF16)
+        d_feeds.push(k, d_feed)
+        add_vectors(
+            k, (1, 4, 5), jnp.sum(d_feed.astype(F32), axis=0, keepdims=True), gain_two_grad, shift_two_grad
+        )
 
     def transpose_rows(i):
         cols = pl.ds(pl.multiple_of(i * 128, 128), 128)
@@ -710,16 +761,21 @@
         for yp, xp in itertools.product(range(2), repeat=2):
             to = pl.ds(pl.multiple_of((i // 4 * 2 + i % 2) * 32, 32), 32)
             N4T[(i // 2) % 2, yp, xp, to, :] = t[yp, xp]
-        C4T[i // 4, (i // 2) % 2, i % 2] = C4[:, cols].astype(F32).T.astype(BF16)
-
-    group_gather(DF4, d_feed, lambda: loop(8, transpose_rows))
-
-    def d_hidden(i):
-        rows = DW[i // 2, i % 2].reshape(TILE, width)
-        cols = col_tile(i)
-        v = (dot(all_rows(DF4), rows, 1, 1) * GP[:, cols]).astype(BF16)
-        DH4[:, cols] = v
-        UB[1:2, cols] = jnp.sum(v.astype(F32), axis=0, keepdims=True)
+        C4T[i // 4, (i // 2) % 2, i % 2] = C4[:, :, :, cols].reshape(group, 128).astype(F32).T.astype(BF16)
+
+    loop(8, transpose_rows)
+
+    def d_hidden(k):
+        def body(i):
+            rows = DW[i // 2, i % 2].reshape(TILE, width)
+            cols = col_tile(i)
+            slope = GP[:, :, rows_of(k), cols].reshape(4 * half_n, TILE)
+            v = (dot(half_rows(DF4, k), rows, 1, 1) * slope).astype(BF16)
+            DH4[:, :, rows_of(k), cols] = v.reshape(2, 2, half_n, TILE)
+            total = jnp.sum(v.astype(F32), axis=0, keepdims=True)
+            UB[1:2, cols] = total if k == 0 else UB[1:2, cols] + total
+
+        loop(hidden // TILE, body)
 
     class Scatter:
         def __init__(self, bufs, product):
@@ -777,7 +833,7 @@
 
     def up_product(dim, v, i):
         rows = N4T[:, :, v] if dim == "x" else N4T[:, v]
-        return dot(rows.reshape(group, group), DH4[:, col_tile(i)])
+        return dot(rows.reshape(group, group), DH4[:, :, :, col_tile(i)].reshape(group, TILE))
 
     def down_product(dim, v, i):
         rows = C4T[:, :, v] if dim == "x" else C4T[:, v]
@@ -791,25 +847,40 @@
     up_s = Scatter((USA, URA, USB, URB, USC, URC, UK), up_product)
     out_s = Scatter((OSA, ORA, OSB, ORB, OSC, ORC, OK), out_product)
 
-    loop(hidden // TILE, d_hidden)
-
     def up_rows(i):
         return UW[i // 2, i % 2].reshape(TILE, hidden)
 
-    d_first = group_sum(
-        (R1A, R1B, R1C, R1D), lambda sp, i: dot(DH4[group_rows(sp), :], up_rows(i), 1, 1), down_s.first
-    )
-    d_sum_one, gain_one_grad, shift_one_grad = norm_backward(
-        DSEC[...] + d_first, NORM1[...], recip_one, gain_one
-    )
-    DSUM[...] = d_sum_one
-    d_branch = d_sum_one.astype(BF16)
-    VG[0:1, :] = jnp.sum(d_branch.astype(F32), axis=0, keepdims=True)
-    VG[2:3, :] = gain_one_grad
-    VG[3:4, :] = shift_one_grad
-    group_gather(DB4, d_branch, up_s.first)
-
-    d_att = dot(all_rows(DB4), OW[...].reshape(4 * HEAD_DIM, width), 1, 1).astype(BF16)
+    d_first = GroupSum((R1A, R1B, R1C, R1D), DH4, lambda left, i: dot(left, up_rows(i), 1, 1))
+    d_branches = GroupGather(DB4)
+    d_feeds.relay(0)
+    d_feeds.pull(0)
+    d_hidden(0)
+    d_feeds.relay(1)
+    d_first.start(0)
+    d_feeds.pull(1)
+    d_hidden(1)
+    d_first.relay(0)
+    d_first.start(1)
+    d_first.relay(1)
+    down_s.first()
+    for k in range(2):
+        r = rows_of(k)
+        d_sum_one, gain_one_grad, shift_one_grad = norm_backward(
+            DSEC[r, :] + d_first.finish(k), NORM1[r, :], recips[k], gain_one
+        )
+        DSUM[r, :] = d_sum_one
+        d_branch = d_sum_one.astype(BF16)
+        d_branches.push(k, d_branch)
+        add_vectors(
+            k, (0, 2, 3), jnp.sum(d_branch.astype(F32), axis=0, keepdims=True), gain_one_grad, shift_one_grad
+        )
+    up_s.first()
+    for k in range(2):
+        d_branches.relay(k)
+    for k in range(2):
+        d_branches.pull(k)
+
+    d_att = dot(DB4[...].reshape(group, width), OW[...].reshape(4 * HEAD_DIM, width), 1, 1).astype(BF16)
     d_att = d_att.astype(F32).T.astype(BF16).reshape(2, 2, HEAD_DIM, group)
     DS[...] = d_att
     d_sem = {f: ids() for f in others}
@@ -867,13 +938,12 @@
         return (C4T if i < tiles // 2 else N4T).at[:, :, :, :, pl.ds(i % 2 * TILE, TILE)]
 
     q1, v1 = attend_back(1)
+    down_s.third()
     up_s.second()
     for i in range(tiles):
         in_sent(i)[...] = input_tile(1, i).astype(BF16)
         send(in_sent(i), IRA.at[i], ia + i, ("s",))
     q0, v0 = attend_back(0)
-    out_s.second()
-
     to_x = Tiles(QSA, QRA, "x", range(tiles))
 
     def q_first(i):
@@ -886,15 +956,16 @@
         QSA[i, :, :, :, 0 : 3 * HEAD_DIM] = QK[i, 1 - x].astype(BF16)
         to_x.send(i)
 
-    for i in range(tiles):
+    in_order = (0, 2, 1, 3)
+    for i in in_order:
         dims = ("l", "y") if i < tiles // 2 else ("y", "l")
         wait(IRA.at[i], ia + i, ("s",))
         IK[i] = input_tile(0, i) + IRA[i].astype(F32)
         ISB[i] = (IK[i, :, 1 - l] if dims[0] == "l" else IK[i, :, :, 1 - y]).astype(BF16)
         send(ISB.at[i], IRB.at[i], ib + i, (dims[0],))
+    up_s.third()
+    out_s.second()
     loop(tiles, q_first)
-    down_s.third()
-
     bq, bv = q0 + q1, v0 + v1
     VG[6:8, :] = jnp.zeros((2, width), F32)
     picked = [spread_matrix(width, 32, j) for j in range(4)]
@@ -925,7 +996,7 @@
     loop(15, lambda j: grad_copy(j + 1).start())
     RG[0] = SG[pl.ds(head * 2, 2)]
 
-    for i in range(tiles):
+    for i in in_order:
         dims = ("l", "y") if i < tiles // 2 else ("y", "l")
         wait(IRB.at[i], ib + i, (dims[0],))
         if dims[0] == "l":
@@ -938,6 +1009,8 @@
             ISC[i] = IK[i, :, 0, 1 - l].astype(BF16)
         send(ISC.at[i], IRC.at[i], ic + i, (dims[1],))
 
+    out_s.third()
+
     def q_second(i):
         to_x.wait(i)
         v = QK[i, x] + QRA[i, :, :, :, 0 : 3 * HEAD_DIM].astype(F32)
@@ -954,8 +1027,13 @@
     loop(15, lambda j: piece_copy(j + 1).start())
     QG[head] = QSB[s, h, l, y]
 
-    up_s.third()
-    out_s.third()
+    for i in in_order:
+        dims = ("l", "y") if i < tiles // 2 else ("y", "l")
+        wait(IRC.at[i], ic + i, (dims[1],))
+        mine_at = y if dims[0] == "l" else l
+        IK[i, :, 1, 0] = IK[i, :, 0, mine_at] + IRC[i].astype(F32)
+        ISD[i] = IK[i, 1 - h, 1, 0].astype(BF16)
+        send(ISD.at[i], IRD.at[i], id_ + i, ("h",))
     down_s.last(downg_o)
     loop(15, lambda j: grad_copy(j + 1).wait_recv())
     small_sum = jnp.sum(RG[...], axis=0)
@@ -975,13 +1053,6 @@
     for hp in range(2):
         upg_o[:, quarter(s, hp, l)] = UF[pl.ds(pl.multiple_of((s * 2 + l) * 32, 32), 32), hp * 512 : (hp + 1) * 512]
 
-    for i in range(tiles):
-        dims = ("l", "y") if i < tiles // 2 else ("y", "l")
-        wait(IRC.at[i], ic + i, (dims[1],))
-        mine_at = y if dims[0] == "l" else l
-        IK[i, :, 1, 0] = IK[i, :, 0, mine_at] + IRC[i].astype(F32)
-        ISD[i] = IK[i, 1 - h, 1, 0].astype(BF16)
-        send(ISD.at[i], IRD.at[i], id_ + i, ("h",))
     out_s.last(outg_o)
 
     wait(RX, x_sem, ("x",))
@@ -1050,7 +1121,7 @@
     def f(*shape):
         return pltpu.VMEM(shape, F32)
 
-    group_bufs = [b(tiles, 2 * n, TILE), b(tiles, 2 * n, TILE), b(tiles, n, TILE), b(tiles, n, TILE)]
+    group_bufs = [b(2, tiles, 2, n // 2, TILE), b(2, tiles, 2, n // 2, TILE), b(2, tiles, n // 2, TILE), b(2, tiles, n // 2, TILE)]
 
     def scatter_bufs(rows):
         return [
@@ -1065,9 +1136,9 @@
         f(8, 128), b(2, 2, 2, 2, n, width), b(HEADS, 32, 256), b(HEADS, 2, 32, 256), f(HEADS, 2, 8, 128),
         b(2, 2, 2, 32, width), b(2, 2, 2, 2, 2, 32, hidden), b(2, 2, 2, 128, width),
         b(2, length, 64), b(2, length, 64), b(2, length, 64), b(2, 192, length), f(2, 64, length), b(2, 64, length),
-        f(2, 8, length), b(4, 2, 64, group // 2), b(2, 2, 64, group), b(group, 256),
-        *group_bufs, *group_bufs, f(tiles, 2, n, TILE),
-        b(2, 2, n, width), b(2, 2, 2, 128, group), b(group, hidden), b(2, 2, 2, 128, group), f(group, hidden),
+        f(2, 8, length), b(4, 2, 64, group // 2), b(2, 2, 64, group), b(2, 2, n, 256),
+        *group_bufs, *group_bufs, f(2, tiles, 2, n // 2, TILE),
+        b(2, 2, n, width), b(2, 2, 2, 128, group), b(2, 2, n, hidden), b(2, 2, 2, 128, group), f(2, 2, n, hidden),
         b(2, 2, n, width),
         f(n, width), f(n, width), f(n, width),
         b(2, 2, 64, group), b(2, 2, 64, group), b(2, length, 64), b(2, 64, length), f(2, length, 64), f(2, 64, length),

time: 226 us -> 210 us (0.929)
  Pallas kernels: 223 us -> 209 us
    pallas_call x1, Pallas kernels: 219 us -> 205 us  [on_block(): pl.pallas_call(layer_kernel, out_shape=shapes, in_specs=[vmem] * 15, out_...]
where the time goes in v3:
time: 210 us
  Pallas kernels  209 us (100%)
    pallas_call x1, Pallas kernels, on_block(): pl.pallas_call(layer_kernel, out_shape=shapes, in_specs=[vmem] * 15, out_...  205 us

profile of v3, /device:TPU:1, one launch (start us, length us, event | category | flops | bytes accessed | tf_op | source)
XLA Modules:
  0.0 209.7 jit_solution(6443949637552131035)
XLA Ops:
  0.7 205.3 %layer.1 = (bf16[128,1024]{1,0:T(8,128)(2,1)}, f32[128,1024]{1,0:T(8,128)}, f32[32,3072]{1,0:T(8,128)}, f32[32,1024]{1,0:T(8,128)}, f32[32,4096]{1,0:T(8,128)}, /*index=5*/f32[128,1024]{1,0:T(8,128)}, f32[8,128]{1,0:T(8,128)}) custom-call(bf16[128,1024]{1,0:T(8,128)(2,1)} %bitcast.22, bf16[32,3072]{1,0:T(8,128)(2,1)} %qkvw.1, bf16[32,1024]{1,0:T(8,128)(2,1)} %outw.1, ...), custom_call_target="tpu_custom_call" | custom-call | tf_op jit(solution)/shard_map/layer/pallas_call | solution.py:1165
  205.9 3.6 %results.1 = (bf16[128,1024]{1,0:T(8,128)(2,1)}, f32[128,1024]{1,0:T(8,128)}, f32[32,3072]{1,0:T(8,128)}, f32[32,1024]{1,0:T(8,128)}, f32[32,4096]{1,0:T(8,128)}...) custom-call(bf16[128,1024]{1,0:T(8,128)(2,1)} %get-tuple-element.37., ...), custom_call_target="tpu_custom_call" | custom-call | tf_op jit(solution)/shard_map/results/pallas_call | solution.py:1178

commit v4 on v3

--- a/solution.py
+++ b/solution.py
@@ -476,8 +476,6 @@
     send(G.at[:, x], G.at[:, x], small_sem[1], ("x",))
     xg[0].pass_on("h", "l")
     xg[1].pass_on("h", "y")
-    for g in dg:
-        g.push(along="hy")
     og.pass_on("h")
     og.pass_on("y")
     og.pass_on("h", "y")
@@ -485,11 +483,9 @@
         g = xg[0] if a == "y" else xg[1]
         for have in ((a,), ("h", a), (b, a), ("h", b, a)):
             g.pass_on(*have)
-    for g in ug:
-        g.pass_on("h")
-    ug[0].pass_on("y")
-    ug[1].pass_on("x")
-
+
+    for g in dg:
+        g.push(along="hy")
     wait(WH.at[:, 1 - x], small_sem[0], ("x",))
     wait(G.at[:, 1 - x], small_sem[1], ("x",))
 
@@ -570,20 +566,20 @@
     project(0)
     attend(0)
     hand_out(0)
-    ug[0].pass_on("h", "y")
-    ug[1].pass_on("h", "x")
+    for g in ug:
+        g.pass_on("h")
+    ug[0].pass_on("y")
+    ug[1].pass_on("x")
     for have in (("s",), ("h", "s"), ("l", "s"), ("h", "l", "s"), ("y", "s"), ("h", "y", "s"), ("l", "y", "s"), ("h", "l", "y", "s")):
         for g in xg:
             g.pull(*have)
     project(1)
     attend(1)
     hand_out(1)
+    ug[0].pass_on("h", "y")
+    ug[1].pass_on("h", "x")
     for g in dg:
         g.pass_on("h")
-    dg[0].pass_on("y")
-    dg[1].pass_on("x")
-    dg[0].pass_on("h", "y")
-    dg[1].pass_on("h", "x")
     for have in (("x",), ("h", "x"), ("y", "x"), ("h", "y", "x")):
         og.pull(*have)
     for flips in others:
@@ -686,6 +682,10 @@
     branch.start(1)
     branch.relay(0)
     branch.relay(1)
+    dg[0].pass_on("y")
+    dg[1].pass_on("x")
+    dg[0].pass_on("h", "y")
+    dg[1].pass_on("h", "x")
 
     normed = GroupGather(N4)
     recips = []
@@ -859,10 +859,10 @@
     d_first.start(0)
     d_feeds.pull(1)
     d_hidden(1)
+    down_s.first()
     d_first.relay(0)
     d_first.start(1)
     d_first.relay(1)
-    down_s.first()
     for k in range(2):
         r = rows_of(k)
         d_sum_one, gain_one_grad, shift_one_grad = norm_backward(
@@ -891,6 +891,26 @@
 
     out_s.first()
     down_s.second()
+    up_s.second()
+
+    VG[6:8, :] = jnp.zeros((2, width), F32)
+    picked = [spread_matrix(width, 32, j) for j in range(4)]
+
+    def exact_pick(row, j):
+        a = jnp.where(mine, VG[row : row + 1, :], 0.0)
+        hi = a.astype(BF16)
+        rest = a - hi.astype(F32)
+        mid = rest.astype(BF16)
+        low = (rest - mid.astype(F32)).astype(BF16)
+        r = picked[j].astype(BF16)
+        return dot(hi, r, 1, 1) + dot(mid, r, 1, 1) + dot(low, r, 1, 1)
+
+    SG[...] = jnp.zeros_like(SG)
+    SG[:, 0, :] = exact_pick(0, 2) + exact_pick(1, 3)
+    SG[:, 1, :] = exact_pick(2, 0) + exact_pick(3, 1) + exact_pick(4, 2) + exact_pick(5, 3)
+    for hp, yp, xp in itertools.product(range(2), repeat=3):
+        r = hp * 4 + yp * 2 + xp
+        SG[(s * 8 + hp * 4 + l * 2 + yp) * 2 + xp, 2:3, :] = UB[1:2, r * 128 : (r + 1) * 128]
 
     for flips in others:
         p = at(flips)
@@ -928,21 +948,25 @@
         DQKVT[j, 128:192, :] = dv.T.astype(BF16)
         return jnp.sum(dq, axis=0, keepdims=True), jnp.sum(dv, axis=0, keepdims=True)
 
-    def input_tile(j, i):
+    def input_tile(j, part, i):
         w = WH[pl.ds(pl.multiple_of(i * 4, 4), 4)].reshape(TILE, WH.shape[-1])[:, 0 : 3 * HEAD_DIM]
-        return dot(DQKV[j], w, 1, 1).reshape(2, 2, 2, tokens, TILE)
-
-    ia, ib, ic, id_ = ([ids() for _ in range(tiles)][0] for _ in range(4))
+        rows = pl.ds(pl.multiple_of(part * (length // 2), length // 2), length // 2)
+        return dot(DQKV[j, rows, :], w, 1, 1).reshape(2, 2, tokens, TILE)
+
+    in_order = (0, 2, 1, 3)
+    far, near = 1 - h, h
+    ia, ib, ic, id_ = ({(p, i): ids() for p in range(2) for i in range(tiles)} for _ in range(4))
 
     def in_sent(i):
         return (C4T if i < tiles // 2 else N4T).at[:, :, :, :, pl.ds(i % 2 * TILE, TILE)]
 
     q1, v1 = attend_back(1)
     down_s.third()
-    up_s.second()
-    for i in range(tiles):
-        in_sent(i)[...] = input_tile(1, i).astype(BF16)
-        send(in_sent(i), IRA.at[i], ia + i, ("s",))
+    for p, part in enumerate((far, near)):
+        for i in in_order:
+            piece = in_sent(i).at[part]
+            piece[...] = input_tile(1, part, i).astype(BF16)
+            send(piece, IRA.at[i, part], ia[p, i], ("s",))
     q0, v0 = attend_back(0)
     to_x = Tiles(QSA, QRA, "x", range(tiles))
 
@@ -956,84 +980,66 @@
         QSA[i, :, :, :, 0 : 3 * HEAD_DIM] = QK[i, 1 - x].astype(BF16)
         to_x.send(i)
 
-    in_order = (0, 2, 1, 3)
-    for i in in_order:
-        dims = ("l", "y") if i < tiles // 2 else ("y", "l")
-        wait(IRA.at[i], ia + i, ("s",))
-        IK[i] = input_tile(0, i) + IRA[i].astype(F32)
-        ISB[i] = (IK[i, :, 1 - l] if dims[0] == "l" else IK[i, :, :, 1 - y]).astype(BF16)
-        send(ISB.at[i], IRB.at[i], ib + i, (dims[0],))
+    def in_second(p):
+        part = (far, near)[p]
+        for i in in_order:
+            wait(IRA.at[i, part], ia[p, i], ("s",))
+            IK[i, part] = input_tile(0, part, i) + IRA[i, part].astype(F32)
+            dim = "l" if i < tiles // 2 else "y"
+            ISB[i, part] = (IK[i, part, 1 - l] if dim == "l" else IK[i, part, :, 1 - y]).astype(BF16)
+            send(ISB.at[i, part], IRB.at[i, part], ib[p, i], (dim,))
+
+    def in_third(p):
+        part = (far, near)[p]
+        for i in in_order:
+            one, two = ("l", "y") if i < tiles // 2 else ("y", "l")
+            wait(IRB.at[i, part], ib[p, i], (one,))
+            IK[i, part, 0] = (IK[i, part, l] if one == "l" else IK[i, part, :, y]) + IRB[i, part].astype(F32)
+            ISC[i, part] = IK[i, part, 0, 1 - here[two]].astype(BF16)
+            send(ISC.at[i, part], IRC.at[i, part], ic[p, i], (two,))
+
+    def in_summed(p, i):
+        part = (far, near)[p]
+        two = "y" if i < tiles // 2 else "l"
+        wait(IRC.at[i, part], ic[p, i], (two,))
+        return IK[i, part, 0, here[two]] + IRC[i, part].astype(F32)
+
+    def q_second(i):
+        to_x.wait(i)
+        v = QK[i, x] + QRA[i, :, :, :, 0 : 3 * HEAD_DIM].astype(F32)
+        QSB[i // 2, i % 2, :, :, :, 0 : 3 * HEAD_DIM] = v.astype(BF16)
+
+    def piece_copy(j):
+        to = (head + j) % 16
+        return peer_copy(
+            QSB.at[to // 8, (to // 4) % 2, (to // 2) % 2, to % 2], QG.at[head], (hss, hrs), 16 + j
+        )
+
+    in_second(0)
+    in_second(1)
     up_s.third()
     out_s.second()
     loop(tiles, q_first)
     bq, bv = q0 + q1, v0 + v1
-    VG[6:8, :] = jnp.zeros((2, width), F32)
-    picked = [spread_matrix(width, 32, j) for j in range(4)]
-
-    def exact_pick(row, j):
-        a = jnp.where(mine, VG[row : row + 1, :], 0.0)
-        hi = a.astype(BF16)
-        rest = a - hi.astype(F32)
-        mid = rest.astype(BF16)
-        low = (rest - mid.astype(F32)).astype(BF16)
-        r = picked[j].astype(BF16)
-        return dot(hi, r, 1, 1) + dot(mid, r, 1, 1) + dot(low, r, 1, 1)
-
-    SG[...] = jnp.zeros_like(SG)
-    SG[:, 0, :] = exact_pick(0, 2) + exact_pick(1, 3)
-    SG[:, 1, :] = exact_pick(2, 0) + exact_pick(3, 1) + exact_pick(4, 2) + exact_pick(5, 3)
     for k in range(2):
         b = head * 2 + k
         lanes = slice(k * 32, k * 32 + 32)
         SG[b, 0:1, :] += jnp.concatenate([bq[:, lanes], bv[:, lanes], jnp.zeros((1, 64), F32)], axis=1)
-    for hp, yp, xp in itertools.product(range(2), repeat=3):
-        r = hp * 4 + yp * 2 + xp
-        SG[(s * 8 + hp * 4 + l * 2 + yp) * 2 + xp, 2:3, :] = UB[1:2, r * 128 : (r + 1) * 128]
 
     def grad_copy(j):
         return peer_copy(SG.at[pl.ds((head + j) % 16 * 2, 2)], RG.at[j], (hss, hrs), j)
 
     loop(15, lambda j: grad_copy(j + 1).start())
     RG[0] = SG[pl.ds(head * 2, 2)]
-
-    for i in in_order:
-        dims = ("l", "y") if i < tiles // 2 else ("y", "l")
-        wait(IRB.at[i], ib + i, (dims[0],))
-        if dims[0] == "l":
-            u = IK[i, :, l] + IRB[i].astype(F32)
-            IK[i, :, 0] = u
-            ISC[i] = IK[i, :, 0, 1 - y].astype(BF16)
-        else:
-            u = IK[i, :, :, y] + IRB[i].astype(F32)
-            IK[i, :, 0] = u
-            ISC[i] = IK[i, :, 0, 1 - l].astype(BF16)
-        send(ISC.at[i], IRC.at[i], ic + i, (dims[1],))
-
+    in_third(0)
     out_s.third()
-
-    def q_second(i):
-        to_x.wait(i)
-        v = QK[i, x] + QRA[i, :, :, :, 0 : 3 * HEAD_DIM].astype(F32)
-        QSB[i // 2, i % 2, :, :, :, 0 : 3 * HEAD_DIM] = v.astype(BF16)
-
     loop(tiles, q_second)
-
-    def piece_copy(j):
-        to = (head + j) % 16
-        return peer_copy(
-            QSB.at[to // 8, (to // 4) % 2, (to // 2) % 2, to % 2], QG.at[head], (hss, hrs), 16 + j
-        )
-
     loop(15, lambda j: piece_copy(j + 1).start())
     QG[head] = QSB[s, h, l, y]
-
     for i in in_order:
-        dims = ("l", "y") if i < tiles // 2 else ("y", "l")
-        wait(IRC.at[i], ic + i, (dims[1],))
-        mine_at = y if dims[0] == "l" else l
-        IK[i, :, 1, 0] = IK[i, :, 0, mine_at] + IRC[i].astype(F32)
-        ISD[i] = IK[i, 1 - h, 1, 0].astype(BF16)
-        send(ISD.at[i], IRD.at[i], id_ + i, ("h",))
+        ISD[i] = in_summed(0, i).astype(BF16)
+        send(ISD.at[i], IRD.at[i], id_[0, i], ("h",))
+    in_third(1)
     down_s.last(downg_o)
     loop(15, lambda j: grad_copy(j + 1).wait_recv())
     small_sum = jnp.sum(RG[...], axis=0)
@@ -1052,12 +1058,9 @@
             )
     for hp in range(2):
         upg_o[:, quarter(s, hp, l)] = UF[pl.ds(pl.multiple_of((s * 2 + l) * 32, 32), 32), hp * 512 : (hp + 1) * 512]
-
     out_s.last(outg_o)
-
     wait(RX, x_sem, ("x",))
     small_o[...] = SX[x] + RX[...]
-
     loop(15, lambda j: piece_copy(j + 1).wait_recv())
     for k in range(HEADS // 2):
         a, b = QG[2 * k].astype(F32), QG[2 * k + 1].astype(F32)
@@ -1065,11 +1068,10 @@
             lanes = slice(part * 64, part * 64 + 64)
             to = part * width + k * 128
             qkvg_o[:, to : to + 128] = jnp.concatenate([a[:, lanes], b[:, lanes]], axis=1)
-
     for i in range(tiles):
-        wait(IRD.at[i], id_ + i, ("h",))
-        cols = slice(i * TILE, (i + 1) * TILE)
-        ig_o[:, cols] = IK[i, h, 1, 0] + IRD[i].astype(F32) + DSUM[:, cols]
+        total = in_summed(1, i) + DSUM[:, i * TILE : (i + 1) * TILE]
+        wait(IRD.at[i], id_[0, i], ("h",))
+        ig_o[:, i * TILE : (i + 1) * TILE] = total + IRD[i].astype(F32)
 
     for flips in (("s",), ("l",), ("s", "l")):
         p = at(flips)

time: 210 us -> 203 us (0.967)
  Pallas kernels: 209 us -> 202 us
    pallas_call x1, Pallas kernels: 205 us -> 198 us  [on_block(): pl.pallas_call(layer_kernel, out_shape=shapes, in_specs=[vmem] * 15, out_...]
where the time goes in v4:
time: 203 us; the launch traced here: 202 us
  Pallas kernels  202 us (100%)
    pallas_call x1, Pallas kernels, on_block(): pl.pallas_call(layer_kernel, out_shape=shapes, in_specs=[vmem] * 15, out_...  198 us

profile of v4, /device:TPU:1, one launch (start us, length us, event | category | flops | bytes accessed | tf_op | source)
XLA Modules:
  0.0 202.5 jit_solution(13120530159563705743)
XLA Ops:
  0.7 198.0 %layer.1 = (bf16[128,1024]{1,0:T(8,128)(2,1)}, f32[128,1024]{1,0:T(8,128)}, f32[32,3072]{1,0:T(8,128)}, f32[32,1024]{1,0:T(8,128)}, f32[32,4096]{1,0:T(8,128)}, /*index=5*/f32[128,1024]{1,0:T(8,128)}, f32[8,128]{1,0:T(8,128)}) custom-call(bf16[128,1024]{1,0:T(8,128)(2,1)} %bitcast.22, bf16[32,3072]{1,0:T(8,128)(2,1)} %qkvw.1, bf16[32,1024]{1,0:T(8,128)(2,1)} %outw.1, ...), custom_call_target="tpu_custom_call" | custom-call | tf_op jit(solution)/shard_map/layer/pallas_call | solution.py:1167
  198.7 3.6 %results.1 = (bf16[128,1024]{1,0:T(8,128)(2,1)}, f32[128,1024]{1,0:T(8,128)}, f32[32,3072]{1,0:T(8,128)}, f32[32,1024]{1,0:T(8,128)}, f32[32,4096]{1,0:T(8,128)}...) custom-call(bf16[128,1024]{1,0:T(8,128)(2,1)} %get-tuple-element.37., ...), custom_call_target="tpu_custom_call" | custom-call | tf_op jit(solution)/shard_map/results/pallas_call | solution.py:1180

commit v5 on v4

--- a/solution.py
+++ b/solution.py
@@ -732,10 +732,10 @@
     feed.start(0)
     normed.pull(1)
     up(1)
+    settle(mark)
     feed.relay(0)
     feed.start(1)
     feed.relay(1)
-    settle(mark)
 
     d_feeds = GroupGather(DF4)
     for k in range(2):
@@ -953,7 +953,7 @@
         rows = pl.ds(pl.multiple_of(part * (length // 2), length // 2), length // 2)
         return dot(DQKV[j, rows, :], w, 1, 1).reshape(2, 2, tokens, TILE)
 
-    in_order = (0, 2, 1, 3)
+    in_order = (0, 1, 2, 3)
     far, near = 1 - h, h
     ia, ib, ic, id_ = ({(p, i): ids() for p in range(2) for i in range(tiles)} for _ in range(4))
 
@@ -985,14 +985,14 @@
         for i in in_order:
             wait(IRA.at[i, part], ia[p, i], ("s",))
             IK[i, part] = input_tile(0, part, i) + IRA[i, part].astype(F32)
-            dim = "l" if i < tiles // 2 else "y"
+            dim = "l" if i < 1 else "y"
             ISB[i, part] = (IK[i, part, 1 - l] if dim == "l" else IK[i, part, :, 1 - y]).astype(BF16)
             send(ISB.at[i, part], IRB.at[i, part], ib[p, i], (dim,))
 
     def in_third(p):
         part = (far, near)[p]
         for i in in_order:
-            one, two = ("l", "y") if i < tiles // 2 else ("y", "l")
+            one, two = ("l", "y") if i < 1 else ("y", "l")
             wait(IRB.at[i, part], ib[p, i], (one,))
             IK[i, part, 0] = (IK[i, part, l] if one == "l" else IK[i, part, :, y]) + IRB[i, part].astype(F32)
             ISC[i, part] = IK[i, part, 0, 1 - here[two]].astype(BF16)
@@ -1000,7 +1000,7 @@
 
     def in_summed(p, i):
         part = (far, near)[p]
-        two = "y" if i < tiles // 2 else "l"
+        two = "y" if i < 1 else "l"
         wait(IRC.at[i, part], ic[p, i], (two,))
         return IK[i, part, 0, here[two]] + IRC[i, part].astype(F32)
 

time: 203 us -> 200 us (0.985)
  Pallas kernels: 202 us -> 199 us
    pallas_call x1, Pallas kernels: 198 us -> 195 us  [on_block(): pl.pallas_call(layer_kernel, out_shape=shapes, in_specs=[vmem] * 15, out_...]
where the time goes in v5:
time: 200 us
  Pallas kernels  199 us (100%)
    pallas_call x1, Pallas kernels, on_block(): pl.pallas_call(layer_kernel, out_shape=shapes, in_specs=[vmem] * 15, out_...  195 us

profile of v5, /device:TPU:1, one launch (start us, length us, event | category | flops | bytes accessed | tf_op | source)
XLA Modules:
  0.0 199.6 jit_solution(18373406316326776743)
XLA Ops:
  0.7 195.2 %layer.1 = (bf16[128,1024]{1,0:T(8,128)(2,1)}, f32[128,1024]{1,0:T(8,128)}, f32[32,3072]{1,0:T(8,128)}, f32[32,1024]{1,0:T(8,128)}, f32[32,4096]{1,0:T(8,128)}, /*index=5*/f32[128,1024]{1,0:T(8,128)}, f32[8,128]{1,0:T(8,128)}) custom-call(bf16[128,1024]{1,0:T(8,128)(2,1)} %bitcast.22, bf16[32,3072]{1,0:T(8,128)(2,1)} %qkvw.1, bf16[32,1024]{1,0:T(8,128)(2,1)} %outw.1, ...), custom_call_target="tpu_custom_call" | custom-call | tf_op jit(solution)/shard_map/layer/pallas_call | solution.py:1167
  195.9 3.6 %results.1 = (bf16[128,1024]{1,0:T(8,128)(2,1)}, f32[128,1024]{1,0:T(8,128)}, f32[32,3072]{1,0:T(8,128)}, f32[32,1024]{1,0:T(8,128)}, f32[32,4096]{1,0:T(8,128)}...) custom-call(bf16[128,1024]{1,0:T(8,128)(2,1)} %get-tuple-element.37., ...), custom_call_target="tpu_custom_call" | custom-call | tf_op jit(solution)/shard_map/results/pallas_call | solution.py:1180

commit v6 on v5

--- a/solution.py
+++ b/solution.py
@@ -441,11 +441,11 @@
             )
 
     def up_block(k):
-        cols = (pl.ds(0, UW.shape[-1] // 2), pl.ds(UW.shape[-1] // 2, UW.shape[-1] // 2))[k]
+        cols = (pl.ds(0, UW.shape[-1] // 8 * 5), pl.ds(UW.shape[-1] // 8 * 5, UW.shape[-1] // 8 * 3))[k]
         return lambda p: UW.at[:, p["h"], :, p["y"], p["x"], :, cols]
 
     def down_block(k):
-        rows = (pl.ds(0, DW.shape[-2] // 2), pl.ds(DW.shape[-2] // 2, DW.shape[-2] // 2))[k]
+        rows = (pl.ds(0, DW.shape[-2] // 8 * 5), pl.ds(DW.shape[-2] // 8 * 5, DW.shape[-2] // 8 * 3))[k]
         return lambda p: DW.at[p["h"], p["y"], p["x"], rows]
 
     og = Gather("hyx", lambda p: OW.at[p["h"], p["y"], p["x"]])
@@ -778,13 +778,13 @@
         loop(hidden // TILE, body)
 
     class Scatter:
-        def __init__(self, bufs, product):
+        def __init__(self, bufs, product, cut=tiles // 2):
             self.sa, self.ra, self.sb, self.rb, self.sc, self.rc, self.keep = bufs
             self.product = product
             self.shape = self.sa.shape[1:]
             self.parts = []
             for k, (one, two) in enumerate((("x", "y"), ("y", "x"))):
-                of = range(k * tiles // 2, (k + 1) * tiles // 2)
+                of = (range(cut), range(cut, tiles))[k]
                 self.parts.append((
                     one, two, of,
                     Tiles(self.sa, self.ra, one, of), Tiles(self.sb, self.rb, two, of), Tiles(self.sc, self.rc, "h", of),
@@ -845,7 +845,7 @@
 
     down_s = Scatter((DSA, DRA, DSB, DRB, DSC, DRC, DK), down_product)
     up_s = Scatter((USA, URA, USB, URB, USC, URC, UK), up_product)
-    out_s = Scatter((OSA, ORA, OSB, ORB, OSC, ORC, OK), out_product)
+    out_s = Scatter((OSA, ORA, OSB, ORB, OSC, ORC, OK), out_product, 3)
 
     def up_rows(i):
         return UW[i // 2, i % 2].reshape(TILE, hidden)

time: 200 us -> 199 us (level)
  no operation moved by 1% of the time
where the time goes in v6:
time: 199 us
  Pallas kernels  198 us (99%)
    pallas_call x1, Pallas kernels, on_block(): pl.pallas_call(layer_kernel, out_shape=shapes, in_specs=[vmem] * 15, out_...  194 us

profile of v6, /device:TPU:1, one launch (start us, length us, event | category | flops | bytes accessed | tf_op | source)
XLA Modules:
  0.0 198.6 jit_solution(8508706147113579838)
XLA Ops:
  0.7 194.2 %layer.1 = (bf16[128,1024]{1,0:T(8,128)(2,1)}, f32[128,1024]{1,0:T(8,128)}, f32[32,3072]{1,0:T(8,128)}, f32[32,1024]{1,0:T(8,128)}, f32[32,4096]{1,0:T(8,128)}, /*index=5*/f32[128,1024]{1,0:T(8,128)}, f32[8,128]{1,0:T(8,128)}) custom-call(bf16[128,1024]{1,0:T(8,128)(2,1)} %bitcast.22, bf16[32,3072]{1,0:T(8,128)(2,1)} %qkvw.1, bf16[32,1024]{1,0:T(8,128)(2,1)} %outw.1, ...), custom_call_target="tpu_custom_call" | custom-call | tf_op jit(solution)/shard_map/layer/pallas_call | solution.py:1167
  194.8 3.6 %results.1 = (bf16[128,1024]{1,0:T(8,128)(2,1)}, f32[128,1024]{1,0:T(8,128)}, f32[32,3072]{1,0:T(8,128)}, f32[32,1024]{1,0:T(8,128)}, f32[32,4096]{1,0:T(8,128)}...) custom-call(bf16[128,1024]{1,0:T(8,128)(2,1)} %get-tuple-element.37., ...), custom_call_target="tpu_custom_call" | custom-call | tf_op jit(solution)/shard_map/results/pallas_call | solution.py:1180
